TPU v7x, 128 devices: a whole 4x4x4 slice. The times are simulated.
128 devices in a mesh: gx: 16 (over z, x), gy: 8 (over y, core).
Axes of the slice: x: 4, y: 4, z: 4, core: 2. Of those that a mesh axis runs over, the one named last changes fastest.
Arguments:
- background: bfloat16 [16384, 8, 512], P(('gx', 'gy')), may hold values from -6 to 6
- col_target: int32 [16384], P(('gx', 'gy')), may hold values from 0 to 255, as said below
- obs_pert: bfloat16 [16384, 512], P(('gx', 'gy')), may hold values from -64 to 64
- innovation: float32 [16384], P(('gx', 'gy')), may hold values from -6 to 6
- obs_rinv: float32 [16384], P(('gx', 'gy')), may hold values from 0.1 to 1
- obs_loc: float32 [2, 16384], P(None, ('gx', 'gy')), may hold values from 0.2 to 1
- obs_patch: int32 [2, 16384], P(None, ('gx', 'gy')), may hold values from 0 to 255, as said below
Outputs:
- analysed: bfloat16 [16384, 8, 512], P(('gx', 'gy'))
Inputs may be any that keep to these rules, and one draw needn't show every extreme that they name: Column c belongs to patch col_target[c], owned by device col_target[c] // 2; patches are dealt to owners to balance observation load, not by geography. Among the 128 columns of one device at most 2 belong to patches of one owner; in every draw one owner gets exactly 2 columns from every device. `obs_patch`: the 2 entries of an observation name different patches. Among the 256 entries of one device at most 4 name patches of one owner; in every draw one owner is named exactly 4 times by every device.
All inputs are finite; a program needn't handle non-finite values. Where the computation divides by a largest or mean magnitude, that divisor is 1e-20 or more.
Results may differ from a plain program's by a relative error of at most 0.0057.
Values may be sent and summed in bfloat16 or wider, within the bound.
No kernel may reach another device: no remote copies, remote signals or barrier semaphores. Data moves between devices by JAX's collectives and lax.ppermute only.
A program may use at most 64 MiB of HBM per device.

v0:
```python
import jax
import jax.numpy as jnp
from jax import lax
from jax.experimental import pallas as pl
from jax.experimental.pallas import tpu as pltpu
from jax.sharding import PartitionSpec as P

AXES = ("gx", "gy")
PATCH_DEV = 2
OCAP = 4
CAP = 2
META = 128
MIB = 1024 * 1024
F32 = jnp.float32
BF16 = jnp.bfloat16


def ranks(owner, owners):
    n = owner.shape[1]
    onehot = lax.broadcasted_iota(jnp.int32, (owners, n), 0) == owner
    earlier = lax.broadcasted_iota(jnp.int32, (n, n), 0) < lax.broadcasted_iota(jnp.int32, (n, n), 1)
    before = jnp.dot(
        onehot.astype(F32).astype(BF16), earlier.astype(F32).astype(BF16), preferred_element_type=F32
    )
    rank = jnp.sum(jnp.where(onehot, before, 0.0), axis=0, keepdims=True)
    return rank.astype(jnp.int32)


def pack_rows_kernel(pert_ref, innov_ref, rinv_ref, loc_ref, patch_ref, target_ref, out_ref, slot_ref):
    obs, members = pert_ref.shape
    slots = out_ref.shape[0]
    owners = slots // OCAP
    patch = jnp.concatenate([patch_ref[0:1, :], patch_ref[1:2, :]], axis=1)
    owner = patch >> 1
    entry_slot = owner * OCAP + ranks(owner, owners)
    root = jnp.sqrt(rinv_ref[...] * loc_ref[...])
    lifted = (root * innov_ref[...]).astype(BF16).astype(F32)
    root = jnp.concatenate([root[0:1, :], root[1:2, :]], axis=1)
    lifted = jnp.concatenate([lifted[0:1, :], lifted[1:2, :]], axis=1)
    tag = ((patch & 1) + 1).astype(F32)

    target = target_ref[...]
    col_owner = target >> 1
    col_rank = ranks(col_owner, owners)
    slot_ref[...] = col_owner * CAP + col_rank
    col_slot = col_owner * OCAP + col_rank
    col_tag = ((target & 1) + 1).astype(F32)

    chosen = lax.broadcasted_iota(jnp.int32, (slots, 2 * obs), 0) == entry_slot
    col_chosen = lax.broadcasted_iota(jnp.int32, (slots, target.shape[1]), 0) == col_slot

    def pick(mask, values):
        return jnp.sum(jnp.where(mask, values, 0.0), axis=1, keepdims=True)

    pick_rows = chosen.astype(F32)
    pick_rows = (pick_rows[:, :obs] + pick_rows[:, obs:]).astype(BF16)
    rows = jnp.dot(pick_rows, pert_ref[...], preferred_element_type=F32)
    out_ref[:, :members] = (rows * pick(chosen, root)).astype(BF16)
    lane = lax.broadcasted_iota(jnp.int32, (slots, META), 1)
    meta = jnp.where(lane == 0, pick(chosen, lifted), 0.0)
    meta = jnp.where(lane == 1, pick(chosen, tag), meta)
    meta = jnp.where(lane == 2, pick(col_chosen, col_tag), meta)
    out_ref[:, members:] = meta.astype(BF16)


def pack_cols_kernel(slot_ref, cols_ref, out_ref, sem):
    count = cols_ref.shape[0]

    def start(i, carry):
        pltpu.make_async_copy(cols_ref.at[i], out_ref.at[slot_ref[0, i]], sem).start()
        return carry

    lax.fori_loop(0, count, start, 0, unroll=8)
    pltpu.make_async_copy(cols_ref, out_ref.at[pl.ds(0, count)], sem).wait()


def unpack_cols_kernel(slot_ref, cols_ref, out_ref, sem):
    count = out_ref.shape[0]

    def start(i, carry):
        pltpu.make_async_copy(cols_ref.at[slot_ref[0, i]], out_ref.at[i], sem).start()
        return carry

    lax.fori_loop(0, count, start, 0, unroll=8)
    pltpu.make_async_copy(cols_ref.at[pl.ds(0, count)], out_ref, sem).wait()


def split(x):
    high = x.astype(BF16)
    return high, (x - high.astype(F32)).astype(BF16)


def product(a, b):
    (ah, al), (bh, bl) = a, b
    return (
        jnp.dot(ah, bh, preferred_element_type=F32)
        + jnp.dot(ah, bl, preferred_element_type=F32)
        + jnp.dot(al, bh, preferred_element_type=F32)
    )


def two_steps(x, diagonal):
    parts = split(x)
    square = product(parts, parts)
    inner = 0.0625 * square - 0.5625 * x + 1.6875 * diagonal
    return product(split(inner), split(square)) - 2.4375 * x + 2.25 * diagonal


def weights_kernel(rows_ref, out_ref):
    members = out_ref.shape[1]
    meta = rows_ref[:, members:].astype(F32)
    tag = meta[:, 1:2]
    rows = rows_ref[...].astype(F32)
    diagonal = (
        lax.broadcasted_iota(jnp.int32, (members, members), 0)
        == lax.broadcasted_iota(jnp.int32, (members, members), 1)
    ).astype(F32)
    for patch in range(PATCH_DEV):
        masked = jnp.where(tag == patch + 1, rows, 0.0).astype(BF16)
        wide = lax.dot_general(
            masked[:, :members], masked, (((0,), (0,)), ((), ())), preferred_element_type=F32
        )
        pull = wide[:, members : members + 1]
        system = wide[:, :members] + (members - 1) * diagonal
        bound = jnp.max(jnp.sum(jnp.abs(system), axis=0, keepdims=True), axis=1, keepdims=True)
        scale = 1.0 / bound
        current = system * scale
        half = two_steps(current, diagonal)
        half_parts = split(half)
        later = product(split(product(half_parts, half_parts)), split(current))
        inverse = product(half_parts, split(two_steps(later, diagonal)))
        once = jnp.sum(inverse * pull, axis=0, keepdims=True)
        mean_weight = jnp.sum(inverse * once, axis=1, keepdims=True) * scale
        out_ref[patch] = (jnp.sqrt((members - 1) * scale) * inverse + mean_weight).astype(BF16)


def apply_kernel(cols_ref, tag_ref, weights_ref, out_ref):
    slots, levels, members = cols_ref.shape
    widened = cols_ref[...].astype(F32)
    mean = jnp.mean(widened, axis=-1, keepdims=True)
    spread = (widened - mean).reshape(slots * levels, members).astype(BF16)
    first = jnp.dot(spread, weights_ref[0], preferred_element_type=F32)
    second = jnp.dot(spread, weights_ref[1], preferred_element_type=F32)
    is_second = tag_ref[...].reshape(slots * levels, -1)[:, 0:1] == 2.0
    increment = jnp.where(is_second, second, first).reshape(slots, levels, members)
    out_ref[...] = (mean + increment).astype(BF16)


def exchange(x):
    return lax.all_to_all(x, AXES, split_axis=0, concat_axis=0, tiled=True)


VMEM = pl.BlockSpec(memory_space=pltpu.VMEM)
SMEM = pl.BlockSpec(memory_space=pltpu.SMEM)
ANY = pl.BlockSpec(memory_space=pl.ANY)


def on_device(background, col_target, obs_pert, innovation, obs_rinv, obs_loc, obs_patch):
    owners = lax.axis_size(AXES)
    cols, levels, members = background.shape
    width = members + META
    payload, col_slot = pl.pallas_call(
        pack_rows_kernel,
        out_shape=(
            jax.ShapeDtypeStruct((owners * OCAP, width), BF16),
            jax.ShapeDtypeStruct((1, cols), jnp.int32),
        ),
        in_specs=[VMEM] * 6,
        out_specs=(VMEM, VMEM),
        name="pack_rows",
    )(
        obs_pert,
        innovation[None, :],
        obs_rinv[None, :],
        obs_loc,
        obs_patch,
        col_target[None, :],
    )
    payload = exchange(payload.reshape(owners, OCAP, width))

    send = pl.pallas_call(
        pack_cols_kernel,
        out_shape=jax.ShapeDtypeStruct((owners * CAP, levels, members), BF16),
        in_specs=[SMEM, ANY],
        out_specs=ANY,
        scratch_shapes=[pltpu.SemaphoreType.DMA],
        name="pack_cols",
        cost_estimate=pl.CostEstimate(flops=0, bytes_accessed=6 * MIB, transcendentals=0),
    )(col_slot, background)
    received = exchange(send.reshape(owners, CAP, levels, members)).reshape(send.shape)

    weights = pl.pallas_call(
        weights_kernel,
        out_shape=jax.ShapeDtypeStruct((PATCH_DEV, members, members), BF16),
        in_specs=[VMEM],
        out_specs=VMEM,
        compiler_params=pltpu.CompilerParams(vmem_limit_bytes=40 * MIB),
        name="weights",
        cost_estimate=pl.CostEstimate(
            flops=2 * 2 * 23 * members**3, bytes_accessed=2 * MIB, transcendentals=0
        ),
    )(payload.reshape(owners * OCAP, width))
    tags = jnp.broadcast_to(
        payload[:, :CAP, members + 2].astype(F32).reshape(owners * CAP, 1, 1),
        (owners * CAP, levels, 128),
    )

    block = 32
    analysed = pl.pallas_call(
        apply_kernel,
        out_shape=jax.ShapeDtypeStruct(send.shape, BF16),
        grid=(send.shape[0] // block,),
        in_specs=[
            pl.BlockSpec((block, levels, members), lambda i: (i, 0, 0)),
            pl.BlockSpec((block, levels, 128), lambda i: (i, 0, 0)),
            pl.BlockSpec((PATCH_DEV, members, members), lambda i: (0, 0, 0)),
        ],
        out_specs=pl.BlockSpec((block, levels, members), lambda i: (i, 0, 0)),
        compiler_params=pltpu.CompilerParams(vmem_limit_bytes=32 * MIB),
        name="apply_weights",
    )(received, tags, weights)

    returned = exchange(analysed.reshape(owners, CAP, levels, members)).reshape(send.shape)
    return pl.pallas_call(
        unpack_cols_kernel,
        out_shape=jax.ShapeDtypeStruct(background.shape, BF16),
        in_specs=[SMEM, ANY],
        out_specs=ANY,
        scratch_shapes=[pltpu.SemaphoreType.DMA],
        name="unpack_cols",
    )(col_slot, returned)


def solution(mesh):
    return jax.shard_map(
        on_device,
        mesh=mesh,
        in_specs=(
            P(AXES, None, None),
            P(AXES),
            P(AXES, None),
            P(AXES),
            P(AXES),
            P(None, AXES),
            P(None, AXES),
        ),
        out_specs=P(AXES, None, None),
        check_vma=False,
    )
```

profile of v0, /device:TPU:1, one launch (start us, length us, event | category | flops | bytes accessed | tf_op | source)
XLA Modules:
  0.0 163.4 jit_solution(443534488463160089)
XLA Ops:
  0.0 2.5 %pack_rows.1 = (bf16[512,640]{1,0:T(8,128)(2,1)}, s32[1,128]{1,0:T(1,128)}) custom-call(bf16[128,512]{1,0:T(8,128)(2,1)} %pert_ref.1, f32[1,128]{1,0:T(1,128)} %bitcast.11, f32[1,128]{1,0:T(1,128)} %bitcast.12, f32[2,128]{1,0:T(2,128)} %loc_ref.1, s32[2,128]{1,0:T(2,128)} %patch_ref.1, s32[1,128]{1,0:T(1,128)} %bitcast.13), custom_call_target="tpu_custom_call" | custom-call | tf_op jit(solution)/shard_map/pack_rows/pallas_call | solution.py:162
  2.5 2.3 %reshape.28 = bf16[128,4,640]{2,1,0:T(4,128)(2,1)} reshape(bf16[512,640]{1,0:T(8,128)(2,1)} %get-tuple-element.8) | data formatting | bytes 1310720 | tf_op jit(solution)/shard_map/reshape | solution.py:179
  4.8 11.5 %all-to-all-start.1 = ((bf16[128,4,640]{2,1,0:T(4,128)(2,1)}), bf16[128,4,640]{2,1,0:T(4,128)(2,1)S(1)}, u32[]{:S(2)}, u32[]{:S(2)}) async-start(bf16[128,4,640]{2,1,0:T(4,128)(2,1)} %reshape.28), calls=%async_computation.1 | async-start | bytes 1310720 | tf_op jit(solution)/shard_map/all_to_all | solution.py:150
  16.3 33.6 %pack_cols.1 = bf16[256,8,512]{2,1,0:T(8,128)(2,1)} custom-call(s32[1,128]{1,0:T(1,128)} %get-tuple-element.7.slot_ref, bf16[128,8,512]{2,1,0:T(8,128)(2,1)} %cols_ref.1), custom_call_target="tpu_custom_call" | custom-call | bytes 6291456 | tf_op jit(solution)/shard_map/pack_cols/pallas_call | solution.py:181
  49.8 0.0 all-to-all-done.1
  49.8 9.8 %all-to-all-start = ((bf16[128,2,8,512]{3,2,1,0:T(8,128)(2,1)}), bf16[128,2,8,512]{3,2,1,0:T(8,128)(2,1)S(1)}, u32[]{:S(2)}, u32[]{:S(2)}) async-start(bf16[128,2,8,512]{3,2,1,0:T(8,128)(2,1)} %bitcast.9), calls=%async_computation | async-start | bytes 4194304 | tf_op jit(solution)/shard_map/all_to_all | solution.py:150
  59.6 0.3 convert_reduce_fusion
  59.9 0.1 reshape.32
  60.1 1.0 reshape.29.rows_ref
  61.1 0.0 copy-start
  61.1 1.1 copy-done
  62.1 14.2 %weights.1.weights_ref = bf16[2,512,512]{2,1,0:T(8,128)(2,1)S(1)} custom-call(bf16[512,640]{1,0:T(8,128)(2,1)S(1)} %copy-done), custom_call_target="tpu_custom_call" | custom-call | flops 12348030976 | bytes 2097152 | tf_op jit(solution)/shard_map/weights/pallas_call | solution.py:192
  76.3 13.8 %all-to-all-done = bf16[128,2,8,512]{3,2,1,0:T(8,128)(2,1)S(1)} async-done(((bf16[128,2,8,512]{3,2,1,0:T(8,128)(2,1)}), bf16[128,2,8,512]{3,2,1,0:T(8,128)(2,1)S(1)}, u32[]{:S(2)}, u32[]{:S(2)}) %all-to-all-start) | async-done | bytes 2097184 | tf_op jit(solution)/shard_map/all_to_all | solution.py:150
  90.1 0.3 broadcast_in_dim.17.tag_ref
  90.5 4.2 %apply_weights.1 = bf16[256,8,512]{2,1,0:T(8,128)(2,1)S(1)} custom-call(bf16[256,8,512]{2,1,0:T(8,128)(2,1)S(1)} %bitcast.7, f32[256,8,128]{2,1,0:T(8,128)S(1)} %broadcast_in_dim.17.tag_ref, bf16[2,512,512]{2,1,0:T(8,128)(2,1)S(1)} %weights.1.weights_ref), custom_call_target="tpu_custom_call" | custom-call | tf_op jit(solution)/shard_map/apply_weights/pallas_call | solution.py:209
  94.6 35.0 %all_to_all.15 = bf16[128,2,8,512]{3,2,1,0:T(8,128)(2,1)} all-to-all(bf16[128,2,8,512]{3,2,1,0:T(8,128)(2,1)S(1)} %bitcast.8), channel_id=1, replica_groups=mesh['gx'=16,'gy'=8] {'gx','gy'}, dimensions={0} | all-to-all | bytes 4194304 | tf_op jit(solution)/shard_map/all_to_all | solution.py:150
  129.7 33.6 %unpack_cols.1 = bf16[128,8,512]{2,1,0:T(8,128)(2,1)} custom-call(s32[1,128]{1,0:T(1,128)} %get-tuple-element.7.slot_ref, bf16[256,8,512]{2,1,0:T(8,128)(2,1)} %bitcast.10), custom_call_target="tpu_custom_call" | custom-call | tf_op jit(solution)/shard_map/unpack_cols/pallas_call | solution.py:224
Async XLA Ops:
  4.8 45.1 %all-to-all-start.1 = ((bf16[128,4,640]{2,1,0:T(4,128)(2,1)}), bf16[128,4,640]{2,1,0:T(4,128)(2,1)S(1)}, u32[]{:S(2)}, u32[]{:S(2)}) async-start(bf16[128,4,640]{2,1,0:T(4,128)(2,1)} %reshape.28), calls=%async_computation.1 | async-start | bytes 1310720 | tf_op jit(solution)/shard_map/all_to_all | solution.py:150
  49.8 40.3 %all-to-all-start = ((bf16[128,2,8,512]{3,2,1,0:T(8,128)(2,1)}), bf16[128,2,8,512]{3,2,1,0:T(8,128)(2,1)S(1)}, u32[]{:S(2)}, u32[]{:S(2)}) async-start(bf16[128,2,8,512]{3,2,1,0:T(8,128)(2,1)} %bitcast.9), calls=%async_computation | async-start | bytes 4194304 | tf_op jit(solution)/shard_map/all_to_all | solution.py:150
  61.1 1.1 copy-start
where the time goes:
time: 164 us; the launch traced here: 163 us
  Pallas kernels  87.9 us (54%)
  blocking collectives  35 us (21%)
  starting transfers between devices  21.3 us (13%)
  waiting for transfers between devices  13.8 us (8%)
  local copies, waits for them, and re-layouts  4.83 us (3%)
    all_to_all x1, blocking collectives, exchange(): return lax.all_to_all(x, AXES, split_axis=0, concat_axis=0, tiled=True)  35 us
    pallas_call x1, Pallas kernels, on_device(): pl.pallas_call(pack_cols_kernel, out_shape=jax.ShapeDtypeStruct((owners *...  33.6 us
    pallas_call x1, Pallas kernels, on_device(): pl.pallas_call(unpack_cols_kernel, out_shape=jax.ShapeDtypeStruct(backgro...  33.6 us
    all_to_all x2, starting transfers between devices, exchange(): return lax.all_to_all(x, AXES, split_axis=0, concat_axis=0, tiled=True)  21.3 us
    pallas_call x1, Pallas kernels, on_device(): pl.pallas_call(weights_kernel, out_shape=jax.ShapeDtypeStruct((PATCH_DEV,...  14.2 us
    all_to_all x2, waiting for transfers between devices, exchange(): return lax.all_to_all(x, AXES, split_axis=0, concat_axis=0, tiled=True)  13.8 us
    pallas_call x1, Pallas kernels, on_device(): pl.pallas_call(apply_kernel, out_shape=jax.ShapeDtypeStruct(send.shape, B...  4.15 us
  transfers between devices with their start and end apart: 2, of which 1 were waited for; matrix products, arithmetic and copies ran while one was open for 1% of the time, Pallas kernels for 29%

commit v1 on v0

--- a/solution.py
+++ b/solution.py
@@ -28,11 +28,11 @@
 
 def pack_rows_kernel(pert_ref, innov_ref, rinv_ref, loc_ref, patch_ref, target_ref, out_ref, slot_ref):
     obs, members = pert_ref.shape
-    slots = out_ref.shape[0]
-    owners = slots // OCAP
+    owners = out_ref.shape[0]
+    padded = 8 * owners
     patch = jnp.concatenate([patch_ref[0:1, :], patch_ref[1:2, :]], axis=1)
     owner = patch >> 1
-    entry_slot = owner * OCAP + ranks(owner, owners)
+    entry_slot = owner * 8 + ranks(owner, owners)
     root = jnp.sqrt(rinv_ref[...] * loc_ref[...])
     lifted = (root * innov_ref[...]).astype(BF16).astype(F32)
     root = jnp.concatenate([root[0:1, :], root[1:2, :]], axis=1)
@@ -43,11 +43,11 @@
     col_owner = target >> 1
     col_rank = ranks(col_owner, owners)
     slot_ref[...] = col_owner * CAP + col_rank
-    col_slot = col_owner * OCAP + col_rank
+    col_slot = col_owner * 8 + col_rank
     col_tag = ((target & 1) + 1).astype(F32)
 
-    chosen = lax.broadcasted_iota(jnp.int32, (slots, 2 * obs), 0) == entry_slot
-    col_chosen = lax.broadcasted_iota(jnp.int32, (slots, target.shape[1]), 0) == col_slot
+    chosen = lax.broadcasted_iota(jnp.int32, (padded, 2 * obs), 0) == entry_slot
+    col_chosen = lax.broadcasted_iota(jnp.int32, (padded, target.shape[1]), 0) == col_slot
 
     def pick(mask, values):
         return jnp.sum(jnp.where(mask, values, 0.0), axis=1, keepdims=True)
@@ -55,34 +55,32 @@
     pick_rows = chosen.astype(F32)
     pick_rows = (pick_rows[:, :obs] + pick_rows[:, obs:]).astype(BF16)
     rows = jnp.dot(pick_rows, pert_ref[...], preferred_element_type=F32)
-    out_ref[:, :members] = (rows * pick(chosen, root)).astype(BF16)
-    lane = lax.broadcasted_iota(jnp.int32, (slots, META), 1)
+    rows = rows * pick(chosen, root)
+    out_ref[:, :, :members] = rows.reshape(owners, 8, members)[:, :OCAP].astype(BF16)
+    lane = lax.broadcasted_iota(jnp.int32, (padded, META), 1)
     meta = jnp.where(lane == 0, pick(chosen, lifted), 0.0)
     meta = jnp.where(lane == 1, pick(chosen, tag), meta)
     meta = jnp.where(lane == 2, pick(col_chosen, col_tag), meta)
-    out_ref[:, members:] = meta.astype(BF16)
-
-
-def pack_cols_kernel(slot_ref, cols_ref, out_ref, sem):
-    count = cols_ref.shape[0]
-
-    def start(i, carry):
-        pltpu.make_async_copy(cols_ref.at[i], out_ref.at[slot_ref[0, i]], sem).start()
+    out_ref[:, :, members:] = meta.reshape(owners, 8, META)[:, :OCAP].astype(BF16)
+
+
+def pack_cols_kernel(slot_ref, cols_ref, out_ref):
+    def place(i, carry):
+        out_ref[slot_ref[0, i]] = cols_ref[i]
         return carry
 
-    lax.fori_loop(0, count, start, 0, unroll=8)
-    pltpu.make_async_copy(cols_ref, out_ref.at[pl.ds(0, count)], sem).wait()
-
-
-def unpack_cols_kernel(slot_ref, cols_ref, out_ref, sem):
-    count = out_ref.shape[0]
-
-    def start(i, carry):
-        pltpu.make_async_copy(cols_ref.at[slot_ref[0, i]], out_ref.at[i], sem).start()
+    lax.fori_loop(0, cols_ref.shape[0], place, 0, unroll=8)
+
+
+def unpack_cols_kernel(slot_ref, cols_ref, out_ref):
+    block = out_ref.shape[0]
+    first = pl.program_id(0) * block
+
+    def place(i, carry):
+        out_ref[i] = cols_ref[slot_ref[0, first + i]]
         return carry
 
-    lax.fori_loop(0, count, start, 0, unroll=8)
-    pltpu.make_async_copy(cols_ref.at[pl.ds(0, count)], out_ref, sem).wait()
+    lax.fori_loop(0, block, place, 0, unroll=8)
 
 
 def split(x):
@@ -152,7 +150,6 @@
 
 VMEM = pl.BlockSpec(memory_space=pltpu.VMEM)
 SMEM = pl.BlockSpec(memory_space=pltpu.SMEM)
-ANY = pl.BlockSpec(memory_space=pl.ANY)
 
 
 def on_device(background, col_target, obs_pert, innovation, obs_rinv, obs_loc, obs_patch):
@@ -162,7 +159,7 @@
     payload, col_slot = pl.pallas_call(
         pack_rows_kernel,
         out_shape=(
-            jax.ShapeDtypeStruct((owners * OCAP, width), BF16),
+            jax.ShapeDtypeStruct((owners, OCAP, width), BF16),
             jax.ShapeDtypeStruct((1, cols), jnp.int32),
         ),
         in_specs=[VMEM] * 6,
@@ -176,14 +173,13 @@
         obs_patch,
         col_target[None, :],
     )
-    payload = exchange(payload.reshape(owners, OCAP, width))
+    payload = exchange(payload)
 
     send = pl.pallas_call(
         pack_cols_kernel,
         out_shape=jax.ShapeDtypeStruct((owners * CAP, levels, members), BF16),
-        in_specs=[SMEM, ANY],
-        out_specs=ANY,
-        scratch_shapes=[pltpu.SemaphoreType.DMA],
+        in_specs=[SMEM, VMEM],
+        out_specs=VMEM,
         name="pack_cols",
         cost_estimate=pl.CostEstimate(flops=0, bytes_accessed=6 * MIB, transcendentals=0),
     )(col_slot, background)
@@ -224,9 +220,9 @@
     return pl.pallas_call(
         unpack_cols_kernel,
         out_shape=jax.ShapeDtypeStruct(background.shape, BF16),
-        in_specs=[SMEM, ANY],
-        out_specs=ANY,
-        scratch_shapes=[pltpu.SemaphoreType.DMA],
+        grid=(cols // block,),
+        in_specs=[SMEM, VMEM],
+        out_specs=pl.BlockSpec((block, levels, members), lambda i: (i, 0, 0)),
         name="unpack_cols",
     )(col_slot, returned)
 

time: 164 us -> 108 us (0.66)
  Pallas kernels: 87.9 us -> 27.1 us
  waiting for transfers between devices: 13.8 us -> 25.9 us
  starting transfers between devices: 21.3 us -> 16.1 us
  local copies, waits for them, and re-layouts: 4.83 us -> 2.53 us
    pallas_call x1, Pallas kernels: 33.6 us -> 2.79 us  [on_device(): pl.pallas_call(pack_cols_kernel, out_shape=jax.ShapeDtypeStruct((owners *...]
    pallas_call x1, Pallas kernels: 33.6 us -> 3.22 us  [on_device(): pl.pallas_call(unpack_cols_kernel, out_shape=jax.ShapeDtypeStruct(backgro...]
    all_to_all x2, waiting for transfers between devices: 13.8 us -> 25.9 us  [exchange(): return lax.all_to_all(x, AXES, split_axis=0, concat_axis=0, tiled=True)]
    all_to_all x2, starting transfers between devices: 21.3 us -> 16.1 us  [exchange(): return lax.all_to_all(x, AXES, split_axis=0, concat_axis=0, tiled=True)]
    reshape x1 -> x0, local copies, waits for them, and re-layouts: 2.29 us -> none  [on_device(): payload = exchange(payload.reshape(owners, OCAP, width))]
  transfers between devices with their start and end apart: 2 -> 2, of which waited for: 1 -> 2; matrix products, arithmetic and copies ran while one was open for 1% -> 1% of each run, Pallas kernels for 29% -> 16%
where the time goes in v1:
time: 108 us; the launch traced here: 107 us
  blocking collectives  35 us (32%)
  Pallas kernels  27.1 us (25%)
  waiting for transfers between devices  25.9 us (24%)
  starting transfers between devices  16.1 us (15%)
  local copies, waits for them, and re-layouts  2.53 us (2%)
    all_to_all x1, blocking collectives, exchange(): return lax.all_to_all(x, AXES, split_axis=0, concat_axis=0, tiled=True)  35 us
    all_to_all x2, waiting for transfers between devices, exchange(): return lax.all_to_all(x, AXES, split_axis=0, concat_axis=0, tiled=True)  25.9 us
    all_to_all x2, starting transfers between devices, exchange(): return lax.all_to_all(x, AXES, split_axis=0, concat_axis=0, tiled=True)  16.1 us
    pallas_call x1, Pallas kernels, on_device(): pl.pallas_call(weights_kernel, out_shape=jax.ShapeDtypeStruct((PATCH_DEV,...  14.2 us
    pallas_call x1, Pallas kernels, on_device(): pl.pallas_call(apply_kernel, out_shape=jax.ShapeDtypeStruct(send.shape, B...  4.15 us
    pallas_call x1, Pallas kernels, on_device(): pl.pallas_call(unpack_cols_kernel, out_shape=jax.ShapeDtypeStruct(backgro...  3.22 us
    pallas_call x1, Pallas kernels, on_device(): pl.pallas_call(pack_rows_kernel, out_shape=(jax.ShapeDtypeStruct((owners,...  2.8 us
    pallas_call x1, Pallas kernels, on_device(): pl.pallas_call(pack_cols_kernel, out_shape=jax.ShapeDtypeStruct((owners *...  2.79 us
  transfers between devices with their start and end apart: 2, of which 2 were waited for; matrix products, arithmetic and copies ran while one was open for 1% of the time, Pallas kernels for 16%

profile of v1, /device:TPU:1, one launch (start us, length us, event | category | flops | bytes accessed | tf_op | source)
XLA Modules:
  0.0 107.1 jit_solution(3069585989245582250)
XLA Ops:
  0.0 2.8 %pack_rows.1 = (bf16[128,4,640]{2,1,0:T(4,128)(2,1)}, s32[1,128]{1,0:T(1,128)}) custom-call(bf16[128,512]{1,0:T(8,128)(2,1)} %pert_ref.1, f32[1,128]{1,0:T(1,128)} %bitcast.11, f32[1,128]{1,0:T(1,128)} %bitcast.12, f32[2,128]{1,0:T(2,128)} %loc_ref.1, s32[2,128]{1,0:T(2,128)} %patch_ref.1, s32[1,128]{1,0:T(1,128)} %bitcast.13), custom_call_target="tpu_custom_call" | custom-call | tf_op jit(solution)/shard_map/pack_rows/pallas_call | solution.py:159
  2.8 11.5 %all-to-all-start.1 = ((bf16[128,4,640]{2,1,0:T(4,128)(2,1)}), bf16[128,4,640]{2,1,0:T(4,128)(2,1)S(1)}, u32[]{:S(2)}, u32[]{:S(2)}) async-start(bf16[128,4,640]{2,1,0:T(4,128)(2,1)} %get-tuple-element.8), calls=%async_computation.1 | async-start | bytes 1310720 | tf_op jit(solution)/shard_map/all_to_all | solution.py:148
  14.3 2.8 %pack_cols.1 = bf16[256,8,512]{2,1,0:T(8,128)(2,1)} custom-call(s32[1,128]{1,0:T(1,128)} %get-tuple-element.7.slot_ref, bf16[128,8,512]{2,1,0:T(8,128)(2,1)} %cols_ref.1), custom_call_target="tpu_custom_call" | custom-call | bytes 6291456 | tf_op jit(solution)/shard_map/pack_cols/pallas_call | solution.py:178
  17.1 12.0 %all-to-all-done.1 = bf16[128,4,640]{2,1,0:T(4,128)(2,1)S(1)} async-done(((bf16[128,4,640]{2,1,0:T(4,128)(2,1)}), bf16[128,4,640]{2,1,0:T(4,128)(2,1)S(1)}, u32[]{:S(2)}, u32[]{:S(2)}) %all-to-all-start.1) | async-done | bytes 655392 | tf_op jit(solution)/shard_map/all_to_all | solution.py:148
  29.1 4.7 %all-to-all-start = ((bf16[128,2,8,512]{3,2,1,0:T(8,128)(2,1)}), bf16[128,2,8,512]{3,2,1,0:T(8,128)(2,1)S(1)}, u32[]{:S(2)}, u32[]{:S(2)}) async-start(bf16[128,2,8,512]{3,2,1,0:T(8,128)(2,1)} %bitcast.9), calls=%async_computation | async-start | bytes 4194304 | tf_op jit(solution)/shard_map/all_to_all | solution.py:148
  33.8 0.3 convert_reduce_fusion
  34.1 0.1 reshape.28
  34.2 1.0 reshape.25.rows_ref
  35.2 0.0 copy-start
  35.2 1.1 %copy-done = bf16[512,640]{1,0:T(8,128)(2,1)S(1)} copy-done((bf16[512,640]{1,0:T(8,128)(2,1)S(1)}, bf16[512,640]{1,0:T(8,128)(2,1)}, u32[]{:S(2)}) %copy-start) | copy-done | bytes 655384
  36.3 14.2 %weights.1.weights_ref = bf16[2,512,512]{2,1,0:T(8,128)(2,1)S(1)} custom-call(bf16[512,640]{1,0:T(8,128)(2,1)S(1)} %copy-done), custom_call_target="tpu_custom_call" | custom-call | flops 12348030976 | bytes 2097152 | tf_op jit(solution)/shard_map/weights/pallas_call | solution.py:188
  50.4 13.9 %all-to-all-done = bf16[128,2,8,512]{3,2,1,0:T(8,128)(2,1)S(1)} async-done(((bf16[128,2,8,512]{3,2,1,0:T(8,128)(2,1)}), bf16[128,2,8,512]{3,2,1,0:T(8,128)(2,1)S(1)}, u32[]{:S(2)}, u32[]{:S(2)}) %all-to-all-start) | async-done | bytes 2097184 | tf_op jit(solution)/shard_map/all_to_all | solution.py:148
  64.4 0.3 broadcast_in_dim.17.tag_ref
  64.7 4.1 %apply_weights.1 = bf16[256,8,512]{2,1,0:T(8,128)(2,1)S(1)} custom-call(bf16[256,8,512]{2,1,0:T(8,128)(2,1)S(1)} %bitcast.7, f32[256,8,128]{2,1,0:T(8,128)S(1)} %broadcast_in_dim.17.tag_ref, bf16[2,512,512]{2,1,0:T(8,128)(2,1)S(1)} %weights.1.weights_ref), custom_call_target="tpu_custom_call" | custom-call | tf_op jit(solution)/shard_map/apply_weights/pallas_call | solution.py:205
  68.9 35.0 %all_to_all.15 = bf16[128,2,8,512]{3,2,1,0:T(8,128)(2,1)} all-to-all(bf16[128,2,8,512]{3,2,1,0:T(8,128)(2,1)S(1)} %bitcast.8), channel_id=1, replica_groups=mesh['gx'=16,'gy'=8] {'gx','gy'}, dimensions={0} | all-to-all | bytes 4194304 | tf_op jit(solution)/shard_map/all_to_all | solution.py:148
  103.9 3.2 %unpack_cols.1 = bf16[128,8,512]{2,1,0:T(8,128)(2,1)} custom-call(s32[1,128]{1,0:T(1,128)} %get-tuple-element.7.slot_ref, bf16[256,8,512]{2,1,0:T(8,128)(2,1)} %bitcast.10), custom_call_target="tpu_custom_call" | custom-call | tf_op jit(solution)/shard_map/unpack_cols/pallas_call | solution.py:220
Async XLA Ops:
  2.8 26.3 %all-to-all-start.1 = ((bf16[128,4,640]{2,1,0:T(4,128)(2,1)}), bf16[128,4,640]{2,1,0:T(4,128)(2,1)S(1)}, u32[]{:S(2)}, u32[]{:S(2)}) async-start(bf16[128,4,640]{2,1,0:T(4,128)(2,1)} %get-tuple-element.8), calls=%async_computation.1 | async-start | bytes 1310720 | tf_op jit(solution)/shard_map/all_to_all | solution.py:148
  29.1 35.3 %all-to-all-start = ((bf16[128,2,8,512]{3,2,1,0:T(8,128)(2,1)}), bf16[128,2,8,512]{3,2,1,0:T(8,128)(2,1)S(1)}, u32[]{:S(2)}, u32[]{:S(2)}) async-start(bf16[128,2,8,512]{3,2,1,0:T(8,128)(2,1)} %bitcast.9), calls=%async_computation | async-start | bytes 4194304 | tf_op jit(solution)/shard_map/all_to_all | solution.py:148
  35.2 1.1 %copy-start = (bf16[512,640]{1,0:T(8,128)(2,1)S(1)}, bf16[512,640]{1,0:T(8,128)(2,1)}, u32[]{:S(2)}) copy-start(bf16[512,640]{1,0:T(8,128)(2,1)} %reshape.25.rows_ref) | copy-start | bytes 1966084

commit v2 on v1

v2 whole, which is shorter than its diff:
```python
import jax
import jax.numpy as jnp
from jax import lax
from jax.experimental import pallas as pl
from jax.experimental.pallas import tpu as pltpu
from jax.sharding import PartitionSpec as P

AXES = ("gx", "gy")
PATCH_DEV = 2
OCAP = 4
CAP = 2
META = 128
MIB = 1024 * 1024
F32 = jnp.float32
BF16 = jnp.bfloat16


def ranks(owner, owners):
    n = owner.shape[1]
    onehot = lax.broadcasted_iota(jnp.int32, (owners, n), 0) == owner
    earlier = lax.broadcasted_iota(jnp.int32, (n, n), 0) < lax.broadcasted_iota(jnp.int32, (n, n), 1)
    before = jnp.dot(
        jnp.where(onehot, 1.0, 0.0).astype(BF16),
        jnp.where(earlier, 1.0, 0.0).astype(BF16),
        preferred_element_type=F32,
    )
    rank = jnp.sum(jnp.where(onehot, before, 0.0), axis=0, keepdims=True)
    return rank.astype(jnp.int32)


def pack_kernel(
    pert_ref, innov_ref, rinv_ref, loc_ref, patch_ref, target_ref, cols_ref, out_ref, slot_ref,
    held_cols, held_slot, cols_sem, slot_sem,
):
    obs, members = pert_ref.shape
    owners = out_ref.shape[0]
    cols = cols_ref.shape[0]
    half = members // 2
    cols_copy = pltpu.make_async_copy(cols_ref, held_cols, cols_sem)
    cols_copy.start()

    target = target_ref[...]
    col_owner = target >> 1
    col_rank = ranks(col_owner, owners)
    slot_ref[...] = col_owner * CAP + col_rank
    slot_copy = pltpu.make_async_copy(slot_ref, held_slot, slot_sem)
    slot_copy.start()

    patch = jnp.concatenate([patch_ref[0:1, :], patch_ref[1:2, :]], axis=1)
    owner = patch >> 1
    entry_slot = owner * 8 + ranks(owner, owners)
    root = jnp.sqrt(rinv_ref[...] * loc_ref[...])
    lifted = root * innov_ref[...]
    root = jnp.concatenate([root[0:1, :], root[1:2, :]], axis=1)
    lifted = jnp.concatenate([lifted[0:1, :], lifted[1:2, :]], axis=1)
    tag = ((patch & 1) + 1).astype(F32)
    col_tag = ((target & 1) + 1).astype(F32)
    col_tags = [jnp.where(col_rank == place, col_tag, 0.0) for place in range(CAP)]
    col_tags = [jnp.concatenate([t, jnp.zeros((1, 2 * obs - cols), F32)], axis=1) for t in col_tags]
    by_entry = jnp.concatenate([root, lifted, tag, *col_tags, jnp.zeros((3, 2 * obs), F32)], axis=0).T

    pert = pert_ref[...].astype(F32)
    rows = (jnp.concatenate([pert, pert], axis=0) * by_entry[:, 0:1]).astype(BF16)
    lane = lax.broadcasted_iota(jnp.int32, (2 * obs, META), 1)
    meta = jnp.where(lane == 0, by_entry[:, 1:2], jnp.where(lane == 1, by_entry[:, 2:3], 0.0))
    lane = lax.broadcasted_iota(jnp.int32, (cols, META), 1)
    col_meta = jnp.where(
        lane == 2, by_entry[:cols, 3:4], jnp.where(lane == 3, by_entry[:cols, 4:5], 0.0)
    )

    place = lax.broadcasted_iota(jnp.int32, (8 * owners, 2 * obs), 0)
    chosen = jnp.where((place & ~OCAP) == entry_slot, 1.0, 0.0).astype(BF16)
    place = lax.broadcasted_iota(jnp.int32, (8 * owners, cols), 0)
    col_chosen = jnp.where((place >> 3) == col_owner, 1.0, 0.0).astype(BF16)
    place = lax.broadcasted_iota(jnp.int32, (8 * owners, half), 0)
    packed = jnp.where(
        (place & OCAP) == 0,
        jnp.dot(chosen, rows[:, :half], preferred_element_type=F32),
        jnp.dot(chosen, rows[:, half:], preferred_element_type=F32),
    )
    out_ref[:, :, 2 * members : 2 * members + half] = packed.reshape(owners, 8, half).astype(BF16)
    packed = jnp.dot(chosen, meta.astype(BF16), preferred_element_type=F32)
    packed += jnp.dot(col_chosen, col_meta.astype(BF16), preferred_element_type=F32)
    out_ref[:, :, 2 * members + half :] = packed.reshape(owners, 8, META).astype(BF16)

    slot_copy.wait()
    cols_copy.wait()

    def put(i, carry):
        slot = held_slot[0, i]
        lanes = pl.ds(pl.multiple_of((slot & 1) * members, members), members)
        out_ref[slot >> 1, :, lanes] = held_cols[i]
        return carry

    lax.fori_loop(0, cols, put, 0, unroll=8)


def unpack_kernel(slot_ref, cols_ref, out_ref):
    block, _, members = out_ref.shape
    first = pl.program_id(0) * block

    def take(i, carry):
        slot = slot_ref[0, first + i]
        lanes = pl.ds(pl.multiple_of((slot & 1) * members, members), members)
        out_ref[i] = cols_ref[slot >> 1, :, lanes]
        return carry

    lax.fori_loop(0, block, take, 0, unroll=8)


def product(a, b):
    return jnp.dot(a.astype(BF16), b.astype(BF16), preferred_element_type=F32)


def two_steps(c, b):
    y = 2.25 + c * (-2.4375 + c * (1.6875 + c * (-0.5625 + c * 0.0625)))
    first = -2.4375 + c * (3.375 + c * (-1.6875 + c * 0.25))
    second = 1.6875 + c * (-1.6875 + c * 0.375)
    third = -0.5625 + c * 0.25
    square = product(b, b)
    return y, product(0.0625 * square + third * b, square) + second * square + first * b


def analyse_kernel(payload_ref, out_ref, weights_ref):
    sources, levels, _ = payload_ref.shape
    members = weights_ref.shape[1]
    half = members // 2
    rows = payload_ref[:, :, 2 * members :].astype(F32).reshape(sources // 2, 2, 8, half + META)
    even, odd = rows[:, 0], rows[:, 1]

    def together(lanes, first):
        pair = [even[:, first : first + OCAP, lanes], odd[:, first : first + OCAP, lanes]]
        return jnp.concatenate(pair, axis=1).reshape(sources * OCAP, -1)

    meta = together(slice(half, half + META), 0)
    tag = meta[:, 1:2]
    rows = jnp.concatenate([together(slice(0, half), 0), together(slice(0, half), OCAP), meta], axis=1)
    diagonal = lax.broadcasted_iota(jnp.int32, (members, members), 0) == lax.broadcasted_iota(
        jnp.int32, (members, members), 1
    )
    for patch in range(PATCH_DEV):
        masked = jnp.where(tag == patch + 1, rows, 0.0).astype(BF16)
        wide = lax.dot_general(
            masked[:, :members], masked, (((0,), (0,)), ((), ())), preferred_element_type=F32
        )
        pull = wide[:, members : members + 1]
        gram = wide[:, :members]
        bound = (members - 1) + jnp.max(
            jnp.sum(jnp.abs(gram), axis=0, keepdims=True), axis=1, keepdims=True
        )
        trace = jnp.sum(jnp.sum(jnp.where(diagonal, gram, 0.0), axis=0, keepdims=True), axis=1, keepdims=True)
        scale = 1.0 / bound
        c = (trace / members + (members - 1)) * scale
        b = gram * scale + jnp.where(diagonal, (members - 1) * scale - c, 0.0)
        z, d = two_steps(c, b)
        u = 2.0 * z * d + product(d, d)
        q = product(u, b) + z * z * b + c * u
        y, f = two_steps(z * z * c, q)
        inverse = product(d, f) + z * f + y * d + jnp.where(diagonal, z * y, 0.0)
        once = jnp.sum(inverse * pull, axis=0, keepdims=True)
        mean_weight = jnp.sum(inverse * once, axis=1, keepdims=True) * scale
        weights_ref[patch] = (jnp.sqrt((members - 1) * scale) * inverse + mean_weight).astype(BF16)

    block = 32
    for place in range(CAP):
        lanes = pl.ds(place * members, members)
        tag_lane = 2 * members + half + 2 + place

        def apply(i, carry):
            some = pl.ds(pl.multiple_of(i * block, block), block)
            widened = payload_ref[some, :, lanes].astype(F32)
            mean = jnp.mean(widened, axis=-1, keepdims=True)
            spread = (widened - mean).reshape(block * levels, members).astype(BF16)
            first = jnp.dot(spread, weights_ref[0], preferred_element_type=F32)
            second = jnp.dot(spread, weights_ref[1], preferred_element_type=F32)
            tags = payload_ref[some, :, pl.ds(2 * members + half, META)].astype(F32)
            tags = tags.reshape(block * levels, META)[:, 2 + place : 3 + place]
            increment = jnp.where(tags == 2.0, second, first).reshape(block, levels, members)
            out_ref[some, :, lanes] = (mean + increment).astype(BF16)
            return carry

        lax.fori_loop(0, sources // block, apply, 0)


def exchange(x):
    return lax.all_to_all(x, AXES, split_axis=0, concat_axis=0, tiled=True)


VMEM = pl.BlockSpec(memory_space=pltpu.VMEM)
SMEM = pl.BlockSpec(memory_space=pltpu.SMEM)
ANY = pl.BlockSpec(memory_space=pl.ANY)


def on_device(background, col_target, obs_pert, innovation, obs_rinv, obs_loc, obs_patch):
    owners = lax.axis_size(AXES)
    cols, levels, members = background.shape
    width = 2 * members + members // 2 + META
    payload, col_slot = pl.pallas_call(
        pack_kernel,
        out_shape=(
            jax.ShapeDtypeStruct((owners, levels, width), BF16),
            jax.ShapeDtypeStruct((1, cols), jnp.int32),
        ),
        in_specs=[VMEM] * 6 + [ANY],
        out_specs=(VMEM, VMEM),
        scratch_shapes=[
            pltpu.VMEM(background.shape, BF16),
            pltpu.SMEM((1, cols), jnp.int32),
            pltpu.SemaphoreType.DMA,
            pltpu.SemaphoreType.DMA,
        ],
        compiler_params=pltpu.CompilerParams(vmem_limit_bytes=32 * MIB),
        name="pack",
    )(
        obs_pert,
        innovation[None, :],
        obs_rinv[None, :],
        obs_loc,
        obs_patch,
        col_target[None, :],
        background,
    )
    payload = exchange(payload)

    analysed = pl.pallas_call(
        analyse_kernel,
        out_shape=jax.ShapeDtypeStruct((owners, levels, CAP * members), BF16),
        in_specs=[VMEM],
        out_specs=VMEM,
        scratch_shapes=[pltpu.VMEM((PATCH_DEV, members, members), BF16)],
        compiler_params=pltpu.CompilerParams(vmem_limit_bytes=40 * MIB),
        name="analyse",
    )(payload)
    returned = exchange(analysed)

    block = 32
    return pl.pallas_call(
        unpack_kernel,
        out_shape=jax.ShapeDtypeStruct(background.shape, BF16),
        grid=(cols // block,),
        in_specs=[SMEM, VMEM],
        out_specs=pl.BlockSpec((block, levels, members), lambda i: (i, 0, 0)),
        name="unpack",
    )(col_slot, returned)


def solution(mesh):
    return jax.shard_map(
        on_device,
        mesh=mesh,
        in_specs=(
            P(AXES, None, None),
            P(AXES),
            P(AXES, None),
            P(AXES),
            P(AXES),
            P(None, AXES),
            P(None, AXES),
        ),
        out_specs=P(AXES, None, None),
        check_vma=False,
    )
```

time: 108 us -> 108 us (level)
  blocking collectives: 35 us -> 85.3 us
  waiting for transfers between devices: 25.9 us -> 0 us
  starting transfers between devices: 16.1 us -> 0 us
  Pallas kernels: 27.1 us -> 16.1 us
  local copies, waits for them, and re-layouts: 2.53 us -> 6.02 us
    all_to_all x1 -> x2, blocking collectives: 35 us -> 85.3 us  [exchange(): return lax.all_to_all(x, AXES, split_axis=0, concat_axis=0, tiled=True)]
    all_to_all x2 -> x0, waiting for transfers between devices: 25.9 us -> none  [exchange(): return lax.all_to_all(x, AXES, split_axis=0, concat_axis=0, tiled=True)]
    all_to_all x2 -> x0, starting transfers between devices: 16.1 us -> none  [exchange(): return lax.all_to_all(x, AXES, split_axis=0, concat_axis=0, tiled=True)]
    pallas_call x5 -> x3, Pallas kernels: 27.1 us -> 16.1 us  [the longest x1 11.2 us: on_device(): pl.pallas_call(analyse_kernel, out_shape=jax.ShapeDtypeStruct((owners, le...]
    unnamed x2 -> x16, local copies, waits for them, and re-layouts: 1.09 us -> 6.02 us
  transfers between devices with their start and end apart: 2 -> 0, of which waited for: 2 -> 0; matrix products, arithmetic and copies ran while one was open for 1% -> 0% of each run, Pallas kernels for 16% -> 0%
where the time goes in v2:
time: 108 us; the launch traced here: 107 us
  blocking collectives  85.3 us (79%)
  Pallas kernels  16.1 us (15%)
  local copies, waits for them, and re-layouts  6.02 us (6%)
    all_to_all x2, blocking collectives, exchange(): return lax.all_to_all(x, AXES, split_axis=0, concat_axis=0, tiled=True)  85.3 us
    pallas_call x1, Pallas kernels, on_device(): pl.pallas_call(analyse_kernel, out_shape=jax.ShapeDtypeStruct((owners, le...  11.2 us
    unnamed x16, local copies, waits for them, and re-layouts  6.02 us
    pallas_call x1, Pallas kernels, on_device(): pl.pallas_call(unpack_kernel, out_shape=jax.ShapeDtypeStruct(background.s...  3.38 us

profile of v2, /device:TPU:1, one launch (start us, length us, event | category | flops | bytes accessed | tf_op | source)
XLA Modules:
  0.0 107.4 jit_solution(12140297775943886461)
XLA Ops:
  0.0 0.0 copy-start
  0.0 1.2 %copy-done = bf16[128,8,512]{2,1,0:T(8,128)(2,1)S(1)} copy-done((bf16[128,8,512]{2,1,0:T(8,128)(2,1)S(1)}, bf16[128,8,512]{2,1,0:T(8,128)(2,1)}, u32[]{:S(2)}) %copy-start) | copy-done | bytes 1048600
  1.2 0.0 copy-start.1
  1.2 0.9 copy-done.1
  2.1 0.0 copy-start.2
  2.1 0.7 copy-done.2
  2.8 0.0 copy-start.3
  2.8 0.7 copy-done.3
  3.5 0.0 copy-start.4
  3.5 0.7 copy-done.4
  4.1 0.0 copy-start.5
  4.1 0.7 copy-done.5
  4.8 0.0 copy-start.6
  4.8 0.7 copy-done.6
  5.5 1.5 %pack.1 = (bf16[128,8,1408]{2,1,0:T(8,128)(2,1)S(1)}, s32[1,128]{1,0:T(1,128)S(1)}) custom-call(bf16[128,512]{1,0:T(8,128)(2,1)S(1)} %copy-done.1, f32[1,128]{1,0:T(1,128)S(1)} %bitcast.3, f32[1,128]{1,0:T(1,128)S(1)} %bitcast.4, f32[2,128]{1,0:T(2,128)S(1)} %copy-done.2, s32[2,128]{1,0:T(2,128)S(1)} %copy-done.3, s32[1,128]{1,0:T(1,128)S(1)} %bitcast.5, ...), custom_call_target="tpu_custom_call" | custom-call | tf_op jit(solution)/shard_map/pack/pallas_call | solution.py:198
  7.0 0.0 copy-start.7
  7.0 0.6 copy-done.7
  7.5 50.3 %all_to_all.10.payload_ref = bf16[128,8,1408]{2,1,0:T(8,128)(2,1)S(1)} all-to-all(bf16[128,8,1408]{2,1,0:T(8,128)(2,1)S(1)} %get-tuple-element.8), channel_id=1, replica_groups=mesh['gx'=16,'gy'=8] {'gx','gy'}, dimensions={0} | all-to-all | bytes 5767168 | tf_op jit(solution)/shard_map/all_to_all | solution.py:186
  57.9 11.2 %analyse.1 = bf16[128,8,1024]{2,1,0:T(8,128)(2,1)S(1)} custom-call(bf16[128,8,1408]{2,1,0:T(8,128)(2,1)S(1)} %all_to_all.10.payload_ref), custom_call_target="tpu_custom_call" | custom-call | tf_op jit(solution)/shard_map/analyse/pallas_call | solution.py:225
  69.0 35.0 %all_to_all.11.cols_ref = bf16[128,8,1024]{2,1,0:T(8,128)(2,1)} all-to-all(bf16[128,8,1024]{2,1,0:T(8,128)(2,1)S(1)} %analyse.1), channel_id=1, replica_groups=mesh['gx'=16,'gy'=8] {'gx','gy'}, dimensions={0} | all-to-all | bytes 4194304 | tf_op jit(solution)/shard_map/all_to_all | solution.py:186
  104.1 3.4 %unpack.1 = bf16[128,8,512]{2,1,0:T(8,128)(2,1)} custom-call(s32[1,128]{1,0:T(1,128)} %copy-done.7, bf16[128,8,1024]{2,1,0:T(8,128)(2,1)} %all_to_all.11.cols_ref), custom_call_target="tpu_custom_call" | custom-call | tf_op jit(solution)/shard_map/unpack/pallas_call | solution.py:237
Async XLA Ops:
  0.0 1.2 %copy-start = (bf16[128,8,512]{2,1,0:T(8,128)(2,1)S(1)}, bf16[128,8,512]{2,1,0:T(8,128)(2,1)}, u32[]{:S(2)}) copy-start(bf16[128,8,512]{2,1,0:T(8,128)(2,1)} %cols_ref.1) | copy-start | bytes 3145732
  1.2 0.9 copy-start.1
  2.1 0.7 copy-start.2
  2.8 0.7 copy-start.3
  3.5 0.7 copy-start.4
  4.1 0.7 copy-start.5
  4.8 0.7 copy-start.6
  7.0 0.6 copy-start.7

commit v3 on v2

--- a/solution.py
+++ b/solution.py
@@ -29,22 +29,35 @@
 
 
 def pack_kernel(
-    pert_ref, innov_ref, rinv_ref, loc_ref, patch_ref, target_ref, cols_ref, out_ref, slot_ref,
-    held_cols, held_slot, cols_sem, slot_sem,
+    pert_hbm, innov_hbm, rinv_hbm, loc_hbm, patch_hbm, target_hbm, cols_hbm, out_ref, slot_hbm,
+    pert_ref, innov_ref, rinv_ref, loc_ref, patch_ref, target_ref, held_cols, slot_ref, held_slot, sems,
 ):
     obs, members = pert_ref.shape
     owners = out_ref.shape[0]
-    cols = cols_ref.shape[0]
+    cols = held_cols.shape[0]
     half = members // 2
-    cols_copy = pltpu.make_async_copy(cols_ref, held_cols, cols_sem)
-    cols_copy.start()
+    pairs = (
+        (target_hbm, target_ref), (patch_hbm, patch_ref), (rinv_hbm, rinv_ref), (loc_hbm, loc_ref),
+        (innov_hbm, innov_ref), (pert_hbm, pert_ref), (cols_hbm, held_cols),
+    )
+    copies = [pltpu.make_async_copy(*pair, sems.at[i]) for i, pair in enumerate(pairs)]
+    for copy in copies:
+        copy.start()
+    target_copy, *row_copies, cols_copy = copies
+    target_copy.wait()
 
     target = target_ref[...]
     col_owner = target >> 1
     col_rank = ranks(col_owner, owners)
     slot_ref[...] = col_owner * CAP + col_rank
-    slot_copy = pltpu.make_async_copy(slot_ref, held_slot, slot_sem)
-    slot_copy.start()
+    slot_copies = [
+        pltpu.make_async_copy(slot_ref, held_slot, sems.at[7]),
+        pltpu.make_async_copy(slot_ref, slot_hbm, sems.at[8]),
+    ]
+    for copy in slot_copies:
+        copy.start()
+    for copy in row_copies:
+        copy.wait()
 
     patch = jnp.concatenate([patch_ref[0:1, :], patch_ref[1:2, :]], axis=1)
     owner = patch >> 1
@@ -83,7 +96,8 @@
     packed += jnp.dot(col_chosen, col_meta.astype(BF16), preferred_element_type=F32)
     out_ref[:, :, 2 * members + half :] = packed.reshape(owners, 8, META).astype(BF16)
 
-    slot_copy.wait()
+    for copy in slot_copies:
+        copy.wait()
     cols_copy.wait()
 
     def put(i, carry):
@@ -95,30 +109,44 @@
     lax.fori_loop(0, cols, put, 0, unroll=8)
 
 
-def unpack_kernel(slot_ref, cols_ref, out_ref):
-    block, _, members = out_ref.shape
-    first = pl.program_id(0) * block
-
-    def take(i, carry):
-        slot = slot_ref[0, first + i]
-        lanes = pl.ds(pl.multiple_of((slot & 1) * members, members), members)
-        out_ref[i] = cols_ref[slot >> 1, :, lanes]
-        return carry
-
-    lax.fori_loop(0, block, take, 0, unroll=8)
+def unpack_kernel(slot_ref, cols_ref, out_hbm, held_cols, sems):
+    cols, _, members = held_cols.shape
+    chunks = sems.shape[0]
+    block = cols // chunks
+    copies = []
+    for chunk in range(chunks):
+
+        def take(i, carry):
+            slot = slot_ref[0, i]
+            lanes = pl.ds(pl.multiple_of((slot & 1) * members, members), members)
+            held_cols[i] = cols_ref[slot >> 1, :, lanes]
+            return carry
+
+        lax.fori_loop(chunk * block, (chunk + 1) * block, take, 0, unroll=8)
+        some = pl.ds(chunk * block, block)
+        copies.append(pltpu.make_async_copy(held_cols.at[some], out_hbm.at[some], sems.at[chunk]))
+        copies[-1].start()
+    for copy in copies:
+        copy.wait()
 
 
 def product(a, b):
     return jnp.dot(a.astype(BF16), b.astype(BF16), preferred_element_type=F32)
 
 
+def products(a, b):
+    return [product(x, y) for x, y in zip(a, b)]
+
+
 def two_steps(c, b):
-    y = 2.25 + c * (-2.4375 + c * (1.6875 + c * (-0.5625 + c * 0.0625)))
-    first = -2.4375 + c * (3.375 + c * (-1.6875 + c * 0.25))
-    second = 1.6875 + c * (-1.6875 + c * 0.375)
-    third = -0.5625 + c * 0.25
-    square = product(b, b)
-    return y, product(0.0625 * square + third * b, square) + second * square + first * b
+    square = products(b, b)
+    y = [2.25 + x * (-2.4375 + x * (1.6875 + x * (-0.5625 + x * 0.0625))) for x in c]
+    first = [-2.4375 + x * (3.375 + x * (-1.6875 + x * 0.25)) for x in c]
+    second = [1.6875 + x * (-1.6875 + x * 0.375) for x in c]
+    third = [-0.5625 + x * 0.25 for x in c]
+    inner = [0.0625 * s + t * x for s, t, x in zip(square, third, b)]
+    high = products(inner, square)
+    return y, [p + t * s + o * x for p, t, s, o, x in zip(high, second, square, first, b)]
 
 
 def analyse_kernel(payload_ref, out_ref, weights_ref):
@@ -138,30 +166,34 @@
     diagonal = lax.broadcasted_iota(jnp.int32, (members, members), 0) == lax.broadcasted_iota(
         jnp.int32, (members, members), 1
     )
-    for patch in range(PATCH_DEV):
-        masked = jnp.where(tag == patch + 1, rows, 0.0).astype(BF16)
-        wide = lax.dot_general(
-            masked[:, :members], masked, (((0,), (0,)), ((), ())), preferred_element_type=F32
-        )
-        pull = wide[:, members : members + 1]
-        gram = wide[:, :members]
-        bound = (members - 1) + jnp.max(
-            jnp.sum(jnp.abs(gram), axis=0, keepdims=True), axis=1, keepdims=True
-        )
-        trace = jnp.sum(jnp.sum(jnp.where(diagonal, gram, 0.0), axis=0, keepdims=True), axis=1, keepdims=True)
-        scale = 1.0 / bound
-        c = (trace / members + (members - 1)) * scale
-        b = gram * scale + jnp.where(diagonal, (members - 1) * scale - c, 0.0)
-        z, d = two_steps(c, b)
-        u = 2.0 * z * d + product(d, d)
-        q = product(u, b) + z * z * b + c * u
-        y, f = two_steps(z * z * c, q)
-        inverse = product(d, f) + z * f + y * d + jnp.where(diagonal, z * y, 0.0)
-        once = jnp.sum(inverse * pull, axis=0, keepdims=True)
-        mean_weight = jnp.sum(inverse * once, axis=1, keepdims=True) * scale
-        weights_ref[patch] = (jnp.sqrt((members - 1) * scale) * inverse + mean_weight).astype(BF16)
-
-    block = 32
+    both = range(PATCH_DEV)
+    masked = [jnp.where(tag == patch + 1, rows, 0.0).astype(BF16) for patch in both]
+    wide = [
+        lax.dot_general(m[:, :members], m, (((0,), (0,)), ((), ())), preferred_element_type=F32)
+        for m in masked
+    ]
+    gram = [w[:, :members] for w in wide]
+    largest = [jnp.sum(jnp.abs(g), axis=0, keepdims=True) for g in gram]
+    bound = [(members - 1) + jnp.max(r, axis=1, keepdims=True) for r in largest]
+    trace = [jnp.sum(jnp.where(diagonal, g, 0.0), axis=0, keepdims=True) for g in gram]
+    trace = [jnp.sum(t, axis=1, keepdims=True) for t in trace]
+    scale = [1.0 / v for v in bound]
+    c = [(t / members + (members - 1)) * v for t, v in zip(trace, scale)]
+    b = [g * v + jnp.where(diagonal, (members - 1) * v - s, 0.0) for g, v, s in zip(gram, scale, c)]
+    z, d = two_steps(c, b)
+    u = [2.0 * zi * di + p for zi, di, p in zip(z, d, products(d, d))]
+    q = [p + zi * zi * bi + ci * ui for p, zi, bi, ci, ui in zip(products(u, b), z, b, c, u)]
+    y, f = two_steps([zi * zi * ci for zi, ci in zip(z, c)], q)
+    last = products(d, f)
+    for patch in both:
+        inverse = last[patch] + z[patch] * f[patch] + y[patch] * d[patch]
+        inverse += jnp.where(diagonal, z[patch] * y[patch], 0.0)
+        once = jnp.sum(inverse * wide[patch][:, members : members + 1], axis=0, keepdims=True)
+        mean_weight = jnp.sum(inverse * once, axis=1, keepdims=True) * scale[patch]
+        root = jnp.sqrt((members - 1) * scale[patch])
+        weights_ref[patch] = (root * inverse + mean_weight).astype(BF16)
+
+    block = 128
     for place in range(CAP):
         lanes = pl.ds(place * members, members)
         tag_lane = 2 * members + half + 2 + place
@@ -188,12 +220,13 @@
 
 VMEM = pl.BlockSpec(memory_space=pltpu.VMEM)
 SMEM = pl.BlockSpec(memory_space=pltpu.SMEM)
-ANY = pl.BlockSpec(memory_space=pl.ANY)
+HBM = pl.BlockSpec(memory_space=pltpu.HBM)
 
 
 def on_device(background, col_target, obs_pert, innovation, obs_rinv, obs_loc, obs_patch):
     owners = lax.axis_size(AXES)
     cols, levels, members = background.shape
+    obs = obs_pert.shape[0]
     width = 2 * members + members // 2 + META
     payload, col_slot = pl.pallas_call(
         pack_kernel,
@@ -201,15 +234,20 @@
             jax.ShapeDtypeStruct((owners, levels, width), BF16),
             jax.ShapeDtypeStruct((1, cols), jnp.int32),
         ),
-        in_specs=[VMEM] * 6 + [ANY],
-        out_specs=(VMEM, VMEM),
+        in_specs=[HBM] * 7,
+        out_specs=(VMEM, HBM),
         scratch_shapes=[
+            pltpu.VMEM(obs_pert.shape, BF16),
+            pltpu.VMEM((1, obs), F32),
+            pltpu.VMEM((1, obs), F32),
+            pltpu.VMEM((2, obs), F32),
+            pltpu.VMEM((2, obs), jnp.int32),
+            pltpu.VMEM((1, cols), jnp.int32),
             pltpu.VMEM(background.shape, BF16),
+            pltpu.VMEM((1, cols), jnp.int32),
             pltpu.SMEM((1, cols), jnp.int32),
-            pltpu.SemaphoreType.DMA,
-            pltpu.SemaphoreType.DMA,
+            pltpu.SemaphoreType.DMA((9,)),
         ],
-        compiler_params=pltpu.CompilerParams(vmem_limit_bytes=32 * MIB),
         name="pack",
     )(
         obs_pert,
@@ -233,13 +271,13 @@
     )(payload)
     returned = exchange(analysed)
 
-    block = 32
     return pl.pallas_call(
         unpack_kernel,
         out_shape=jax.ShapeDtypeStruct(background.shape, BF16),
-        grid=(cols // block,),
         in_specs=[SMEM, VMEM],
-        out_specs=pl.BlockSpec((block, levels, members), lambda i: (i, 0, 0)),
+        out_specs=HBM,
+        scratch_shapes=[pltpu.VMEM(background.shape, BF16), pltpu.SemaphoreType.DMA((4,))],
+        compiler_params=pltpu.CompilerParams(vmem_limit_bytes=16 * MIB),
         name="unpack",
     )(col_slot, returned)
 

time: 108 us -> 99.4 us (0.920)
  local copies, waits for them, and re-layouts: 6.02 us -> 0.01 us
  Pallas kernels: 16.1 us -> 14.3 us
    unnamed x16 -> x2, local copies, waits for them, and re-layouts: 6.02 us -> 0.01 us
    pallas_call x1, Pallas kernels: 11.2 us -> 8.67 us  [on_device(): pl.pallas_call(analyse_kernel, out_shape=jax.ShapeDtypeStruct((owners, le...]
    pallas_call x1, Pallas kernels: 1.5 us -> 3.97 us  [on_device(): pl.pallas_call(pack_kernel, out_shape=(jax.ShapeDtypeStruct((owners, leve...]
    pallas_call x1, Pallas kernels: 3.38 us -> 1.67 us  [on_device(): pl.pallas_call(unpack_kernel, out_shape=jax.ShapeDtypeStruct(background.s...]
where the time goes in v3:
time: 99.4 us; the launch traced here: 99.2 us
  blocking collectives  84.9 us (85%)
  Pallas kernels  14.3 us (14%)
    all_to_all x2, blocking collectives, exchange(): return lax.all_to_all(x, AXES, split_axis=0, concat_axis=0, tiled=True)  84.9 us
    pallas_call x1, Pallas kernels, on_device(): pl.pallas_call(analyse_kernel, out_shape=jax.ShapeDtypeStruct((owners, le...  8.67 us
    pallas_call x1, Pallas kernels, on_device(): pl.pallas_call(pack_kernel, out_shape=(jax.ShapeDtypeStruct((owners, leve...  3.97 us

profile of v3, /device:TPU:1, one launch (start us, length us, event | category | flops | bytes accessed | tf_op | source)
XLA Modules:
  0.0 99.2 jit_solution(9413729727287034150)
XLA Ops:
  0.0 4.0 %pack.1 = (bf16[128,8,1408]{2,1,0:T(8,128)(2,1)}, s32[1,128]{1,0:T(1,128)}) custom-call(bf16[128,512]{1,0:T(8,128)(2,1)} %pert_hbm.1, f32[1,128]{1,0:T(1,128)} %bitcast.3, f32[1,128]{1,0:T(1,128)} %bitcast.4, f32[2,128]{1,0:T(2,128)} %loc_hbm.1, s32[2,128]{1,0:T(2,128)} %patch_hbm.1, s32[1,128]{1,0:T(1,128)} %bitcast.5, bf16[128,8,512]{2,1,0:T(8,128)(2,1)} %cols_hbm.1), custom_call_target="tpu_custom_call" | custom-call | tf_op jit(solution)/shard_map/pack/pallas_call | solution.py:231
  4.0 50.5 %all_to_all.10.payload_ref = bf16[128,8,1408]{2,1,0:T(8,128)(2,1)S(1)} all-to-all(bf16[128,8,1408]{2,1,0:T(8,128)(2,1)} %get-tuple-element.8), channel_id=1, replica_groups=mesh['gx'=16,'gy'=8] {'gx','gy'}, dimensions={0} | all-to-all | bytes 5767168 | tf_op jit(solution)/shard_map/all_to_all | solution.py:218
  54.5 8.7 %analyse.1 = bf16[128,8,1024]{2,1,0:T(8,128)(2,1)S(1)} custom-call(bf16[128,8,1408]{2,1,0:T(8,128)(2,1)S(1)} %all_to_all.10.payload_ref), custom_call_target="tpu_custom_call" | custom-call | tf_op jit(solution)/shard_map/analyse/pallas_call | solution.py:263
  63.2 0.0 copy-start
  63.2 34.3 %all_to_all.11.cols_ref = bf16[128,8,1024]{2,1,0:T(8,128)(2,1)S(1)} all-to-all(bf16[128,8,1024]{2,1,0:T(8,128)(2,1)S(1)} %analyse.1), channel_id=1, replica_groups=mesh['gx'=16,'gy'=8] {'gx','gy'}, dimensions={0} | all-to-all | bytes 4194304 | tf_op jit(solution)/shard_map/all_to_all | solution.py:218
  97.5 0.0 copy-done
  97.5 1.7 %unpack.1 = bf16[128,8,512]{2,1,0:T(8,128)(2,1)} custom-call(s32[1,128]{1,0:T(1,128)S(1)} %copy-done, bf16[128,8,1024]{2,1,0:T(8,128)(2,1)S(1)} %all_to_all.11.cols_ref), custom_call_target="tpu_custom_call" | custom-call | tf_op jit(solution)/shard_map/unpack/pallas_call | solution.py:274
Async XLA Ops:
  63.2 34.4 %copy-start = (s32[1,128]{1,0:T(1,128)S(1)}, s32[1,128]{1,0:T(1,128)}, u32[]{:S(2)}) copy-start(s32[1,128]{1,0:T(1,128)} %get-tuple-element.7.slot_ref) | copy-start | bytes 1540

commit v4 on v3

--- a/solution.py
+++ b/solution.py
@@ -9,10 +9,16 @@
 PATCH_DEV = 2
 OCAP = 4
 CAP = 2
-META = 128
+LANES = 128
 MIB = 1024 * 1024
 F32 = jnp.float32
 BF16 = jnp.bfloat16
+
+GROUPS = 4
+COL_ROWS = (0, 48)
+OBS_ROWS = 32
+META_ROWS = 80
+BLOCK_ROWS = 82
 
 
 def ranks(owner, owners):
@@ -29,13 +35,14 @@
 
 
 def pack_kernel(
-    pert_hbm, innov_hbm, rinv_hbm, loc_hbm, patch_hbm, target_hbm, cols_hbm, out_ref, slot_hbm,
-    pert_ref, innov_ref, rinv_ref, loc_ref, patch_ref, target_ref, held_cols, slot_ref, held_slot, sems,
+    pert_hbm, innov_hbm, rinv_hbm, loc_hbm, patch_hbm, target_hbm, cols_hbm, out_hbm, slot_hbm,
+    pert_ref, innov_ref, rinv_ref, loc_ref, patch_ref, target_ref, held_cols, out_ref, slot_ref,
+    order_ref, held_order, sems, out_sems,
 ):
     obs, members = pert_ref.shape
     owners = out_ref.shape[0]
     cols = held_cols.shape[0]
-    half = members // 2
+    block_ref = out_ref.reshape(owners, BLOCK_ROWS, LANES)
     pairs = (
         (target_hbm, target_ref), (patch_hbm, patch_ref), (rinv_hbm, rinv_ref), (loc_hbm, loc_ref),
         (innov_hbm, innov_ref), (pert_hbm, pert_ref), (cols_hbm, held_cols),
@@ -50,8 +57,13 @@
     col_owner = target >> 1
     col_rank = ranks(col_owner, owners)
     slot_ref[...] = col_owner * CAP + col_rank
+    slot_col = jnp.broadcast_to((col_owner * CAP + col_rank).astype(F32), (8, cols)).T[:, 0:1]
+    places = lax.broadcasted_iota(jnp.int32, (cols, CAP * owners), 1).astype(F32)
+    column = lax.broadcasted_iota(jnp.int32, (cols, CAP * owners), 0).astype(F32)
+    order = jnp.sum(jnp.where(places == slot_col, column, 0.0), axis=0, keepdims=True)
+    order_ref[...] = order.astype(jnp.int32)
     slot_copies = [
-        pltpu.make_async_copy(slot_ref, held_slot, sems.at[7]),
+        pltpu.make_async_copy(order_ref, held_order, sems.at[7]),
         pltpu.make_async_copy(slot_ref, slot_hbm, sems.at[8]),
     ]
     for copy in slot_copies:
@@ -61,52 +73,65 @@
 
     patch = jnp.concatenate([patch_ref[0:1, :], patch_ref[1:2, :]], axis=1)
     owner = patch >> 1
-    entry_slot = owner * 8 + ranks(owner, owners)
+    rank = ranks(owner, owners)
     root = jnp.sqrt(rinv_ref[...] * loc_ref[...])
     lifted = root * innov_ref[...]
     root = jnp.concatenate([root[0:1, :], root[1:2, :]], axis=1)
     lifted = jnp.concatenate([lifted[0:1, :], lifted[1:2, :]], axis=1)
     tag = ((patch & 1) + 1).astype(F32)
     col_tag = ((target & 1) + 1).astype(F32)
-    col_tags = [jnp.where(col_rank == place, col_tag, 0.0) for place in range(CAP)]
-    col_tags = [jnp.concatenate([t, jnp.zeros((1, 2 * obs - cols), F32)], axis=1) for t in col_tags]
-    by_entry = jnp.concatenate([root, lifted, tag, *col_tags, jnp.zeros((3, 2 * obs), F32)], axis=0).T
+    rest = jnp.zeros((1, 2 * obs - cols), F32)
+    col_lane = jnp.concatenate([(col_rank + 8).astype(F32), rest], axis=1)
+    col_tag = jnp.concatenate([col_tag, rest], axis=1)
+    nothing = jnp.zeros((2, 2 * obs), F32)
+    by_entry = jnp.concatenate([root, lifted, tag, rank.astype(F32), col_lane, col_tag, nothing], axis=0).T
 
     pert = pert_ref[...].astype(F32)
     rows = (jnp.concatenate([pert, pert], axis=0) * by_entry[:, 0:1]).astype(BF16)
-    lane = lax.broadcasted_iota(jnp.int32, (2 * obs, META), 1)
-    meta = jnp.where(lane == 0, by_entry[:, 1:2], jnp.where(lane == 1, by_entry[:, 2:3], 0.0))
-    lane = lax.broadcasted_iota(jnp.int32, (cols, META), 1)
-    col_meta = jnp.where(
-        lane == 2, by_entry[:cols, 3:4], jnp.where(lane == 3, by_entry[:cols, 4:5], 0.0)
-    )
+    lane = lax.broadcasted_iota(jnp.int32, (2 * obs, LANES), 1).astype(F32)
+    meta = jnp.where(lane == by_entry[:, 3:4], by_entry[:, 1:2], 0.0)
+    meta = jnp.where(lane == by_entry[:, 3:4] + OCAP, by_entry[:, 2:3], meta)
+    lane = lax.broadcasted_iota(jnp.int32, (cols, LANES), 1).astype(F32)
+    col_meta = jnp.where(lane == by_entry[:cols, 4:5], by_entry[:cols, 5:6], 0.0)
 
     place = lax.broadcasted_iota(jnp.int32, (8 * owners, 2 * obs), 0)
-    chosen = jnp.where((place & ~OCAP) == entry_slot, 1.0, 0.0).astype(BF16)
+    chosen = jnp.where((place & ~OCAP) == owner * 8 + rank, 1.0, 0.0).astype(BF16)
+    packed = jnp.dot(chosen, rows, preferred_element_type=F32)
+    lower = (lax.broadcasted_iota(jnp.int32, (8 * owners, LANES), 0) & OCAP) == 0
+    for pair in range(GROUPS // 2):
+        first = 2 * pair * LANES
+        both = jnp.where(lower, packed[:, first : first + LANES], packed[:, first + LANES : first + 2 * LANES])
+        block_ref[:, OBS_ROWS + 8 * pair : OBS_ROWS + 8 * pair + 8, :] = both.reshape(owners, 8, LANES).astype(BF16)
+    chosen = jnp.where((place >> 3) == owner, 1.0, 0.0).astype(BF16)
     place = lax.broadcasted_iota(jnp.int32, (8 * owners, cols), 0)
     col_chosen = jnp.where((place >> 3) == col_owner, 1.0, 0.0).astype(BF16)
-    place = lax.broadcasted_iota(jnp.int32, (8 * owners, half), 0)
-    packed = jnp.where(
-        (place & OCAP) == 0,
-        jnp.dot(chosen, rows[:, :half], preferred_element_type=F32),
-        jnp.dot(chosen, rows[:, half:], preferred_element_type=F32),
-    )
-    out_ref[:, :, 2 * members : 2 * members + half] = packed.reshape(owners, 8, half).astype(BF16)
     packed = jnp.dot(chosen, meta.astype(BF16), preferred_element_type=F32)
     packed += jnp.dot(col_chosen, col_meta.astype(BF16), preferred_element_type=F32)
-    out_ref[:, :, 2 * members + half :] = packed.reshape(owners, 8, META).astype(BF16)
+    block_ref[:, META_ROWS:, :] = packed.reshape(owners, 8, LANES)[:, : BLOCK_ROWS - META_ROWS].astype(BF16)
 
     for copy in slot_copies:
         copy.wait()
     cols_copy.wait()
 
-    def put(i, carry):
-        slot = held_slot[0, i]
-        lanes = pl.ds(pl.multiple_of((slot & 1) * members, members), members)
-        out_ref[slot >> 1, :, lanes] = held_cols[i]
-        return carry
-
-    lax.fori_loop(0, cols, put, 0, unroll=8)
+    chunks = out_sems.shape[0]
+    block = owners // chunks
+    copies = []
+    for chunk in range(chunks):
+
+        def put(i, carry):
+            for place in range(CAP):
+                column = held_cols[held_order[0, CAP * i + place]]
+                for group in range(GROUPS):
+                    first = COL_ROWS[place] + 8 * group
+                    block_ref[i, first : first + 8, :] = column[:, group * LANES : (group + 1) * LANES]
+            return carry
+
+        lax.fori_loop(chunk * block, (chunk + 1) * block, put, 0, unroll=8)
+        some = pl.ds(chunk * block, block)
+        copies.append(pltpu.make_async_copy(out_ref.at[some], out_hbm.at[some], out_sems.at[chunk]))
+        copies[-1].start()
+    for copy in copies:
+        copy.wait()
 
 
 def unpack_kernel(slot_ref, cols_ref, out_hbm, held_cols, sems):
@@ -150,27 +175,38 @@
 
 
 def analyse_kernel(payload_ref, out_ref, weights_ref):
-    sources, levels, _ = payload_ref.shape
+    sources, levels, _ = out_ref.shape
     members = weights_ref.shape[1]
-    half = members // 2
-    rows = payload_ref[:, :, 2 * members :].astype(F32).reshape(sources // 2, 2, 8, half + META)
-    even, odd = rows[:, 0], rows[:, 1]
-
-    def together(lanes, first):
-        pair = [even[:, first : first + OCAP, lanes], odd[:, first : first + OCAP, lanes]]
-        return jnp.concatenate(pair, axis=1).reshape(sources * OCAP, -1)
-
-    meta = together(slice(half, half + META), 0)
-    tag = meta[:, 1:2]
-    rows = jnp.concatenate([together(slice(0, half), 0), together(slice(0, half), OCAP), meta], axis=1)
+    block_ref = payload_ref.reshape(sources, BLOCK_ROWS, LANES)
+    meta = block_ref[:, META_ROWS:, :].astype(F32)[:, 0:1, :]
+    meta = jnp.broadcast_to(meta, (sources, 8, LANES))
+    col_tags = meta.reshape(sources * 8, LANES)
+
+    half = sources // 2
+    sublane = lax.broadcasted_iota(jnp.int32, (half, 8, LANES), 1)
+    lane = lax.broadcasted_iota(jnp.int32, (half, 8, LANES), 2)
+
+    def together(first):
+        lower = block_ref[:half, first : first + 8, :].astype(F32)
+        upper = block_ref[half:, first - OCAP : first - OCAP + 8, :].astype(F32)
+        return jnp.where(sublane < OCAP, lower, upper).reshape(half * 8, LANES)
+
+    row_meta = jnp.where(sublane < OCAP, meta[:half], meta[half:])
+    row_meta = jnp.where((lane & (OCAP - 1)) == (sublane & (OCAP - 1)), row_meta, 0.0)
+    row_meta = row_meta.reshape(half * 8, LANES)
+    rows = jnp.concatenate([together(OBS_ROWS + OCAP * j) for j in range(GROUPS)] + [row_meta], axis=1)
     diagonal = lax.broadcasted_iota(jnp.int32, (members, members), 0) == lax.broadcasted_iota(
         jnp.int32, (members, members), 1
     )
     both = range(PATCH_DEV)
-    masked = [jnp.where(tag == patch + 1, rows, 0.0).astype(BF16) for patch in both]
+    flipped = rows.T
+    tag = jnp.sum(flipped[members + OCAP : members + 2 * OCAP], axis=0, keepdims=True)
+    rows = rows.astype(BF16)
     wide = [
-        lax.dot_general(m[:, :members], m, (((0,), (0,)), ((), ())), preferred_element_type=F32)
-        for m in masked
+        jnp.dot(
+            jnp.where(tag == patch + 1, flipped[:members], 0.0).astype(BF16), rows, preferred_element_type=F32
+        )
+        for patch in both
     ]
     gram = [w[:, :members] for w in wide]
     largest = [jnp.sum(jnp.abs(g), axis=0, keepdims=True) for g in gram]
@@ -188,30 +224,24 @@
     for patch in both:
         inverse = last[patch] + z[patch] * f[patch] + y[patch] * d[patch]
         inverse += jnp.where(diagonal, z[patch] * y[patch], 0.0)
-        once = jnp.sum(inverse * wide[patch][:, members : members + 1], axis=0, keepdims=True)
+        pull = jnp.sum(wide[patch][:, members : members + OCAP], axis=1, keepdims=True)
+        once = jnp.sum(inverse * pull, axis=0, keepdims=True)
         mean_weight = jnp.sum(inverse * once, axis=1, keepdims=True) * scale[patch]
         root = jnp.sqrt((members - 1) * scale[patch])
         weights_ref[patch] = (root * inverse + mean_weight).astype(BF16)
 
-    block = 128
     for place in range(CAP):
-        lanes = pl.ds(place * members, members)
-        tag_lane = 2 * members + half + 2 + place
-
-        def apply(i, carry):
-            some = pl.ds(pl.multiple_of(i * block, block), block)
-            widened = payload_ref[some, :, lanes].astype(F32)
-            mean = jnp.mean(widened, axis=-1, keepdims=True)
-            spread = (widened - mean).reshape(block * levels, members).astype(BF16)
-            first = jnp.dot(spread, weights_ref[0], preferred_element_type=F32)
-            second = jnp.dot(spread, weights_ref[1], preferred_element_type=F32)
-            tags = payload_ref[some, :, pl.ds(2 * members + half, META)].astype(F32)
-            tags = tags.reshape(block * levels, META)[:, 2 + place : 3 + place]
-            increment = jnp.where(tags == 2.0, second, first).reshape(block, levels, members)
-            out_ref[some, :, lanes] = (mean + increment).astype(BF16)
-            return carry
-
-        lax.fori_loop(0, sources // block, apply, 0)
+        groups = [
+            block_ref[:, COL_ROWS[place] + 8 * j : COL_ROWS[place] + 8 * j + 8, :].astype(F32) for j in range(GROUPS)
+        ]
+        widened = jnp.concatenate(groups, axis=2)
+        mean = jnp.mean(widened, axis=-1, keepdims=True)
+        spread = (widened - mean).reshape(sources * levels, members).astype(BF16)
+        first = jnp.dot(spread, weights_ref[0], preferred_element_type=F32)
+        second = jnp.dot(spread, weights_ref[1], preferred_element_type=F32)
+        increment = jnp.where(col_tags[:, 8 + place : 9 + place] == 2.0, second, first)
+        increment = increment.reshape(sources, levels, members)
+        out_ref[:, :, place * members : (place + 1) * members] = (mean + increment).astype(BF16)
 
 
 def exchange(x):
@@ -227,15 +257,15 @@
     owners = lax.axis_size(AXES)
     cols, levels, members = background.shape
     obs = obs_pert.shape[0]
-    width = 2 * members + members // 2 + META
+    block = (owners, BLOCK_ROWS // 2, 2, LANES)
     payload, col_slot = pl.pallas_call(
         pack_kernel,
         out_shape=(
-            jax.ShapeDtypeStruct((owners, levels, width), BF16),
+            jax.ShapeDtypeStruct(block, BF16),
             jax.ShapeDtypeStruct((1, cols), jnp.int32),
         ),
         in_specs=[HBM] * 7,
-        out_specs=(VMEM, HBM),
+        out_specs=(HBM, HBM),
         scratch_shapes=[
             pltpu.VMEM(obs_pert.shape, BF16),
             pltpu.VMEM((1, obs), F32),
@@ -244,9 +274,12 @@
             pltpu.VMEM((2, obs), jnp.int32),
             pltpu.VMEM((1, cols), jnp.int32),
             pltpu.VMEM(background.shape, BF16),
+            pltpu.VMEM(block, BF16),
             pltpu.VMEM((1, cols), jnp.int32),
-            pltpu.SMEM((1, cols), jnp.int32),
+            pltpu.VMEM((1, CAP * owners), jnp.int32),
+            pltpu.SMEM((1, CAP * owners), jnp.int32),
             pltpu.SemaphoreType.DMA((9,)),
+            pltpu.SemaphoreType.DMA((4,)),
         ],
         name="pack",
     )(

time: 99.4 us -> 99.1 us (level)
  blocking collectives: 84.9 us -> 82.7 us
  Pallas kernels: 14.3 us -> 16.1 us
    all_to_all x2, blocking collectives: 84.9 us -> 82.7 us  [exchange(): return lax.all_to_all(x, AXES, split_axis=0, concat_axis=0, tiled=True)]
    pallas_call x1, Pallas kernels: 8.67 us -> 9.81 us  [on_device(): pl.pallas_call(analyse_kernel, out_shape=jax.ShapeDtypeStruct((owners, le...]
where the time goes in v4:
time: 99.1 us; the launch traced here: 98.8 us
  blocking collectives  82.7 us (83%)
  Pallas kernels  16.1 us (16%)
    all_to_all x2, blocking collectives, exchange(): return lax.all_to_all(x, AXES, split_axis=0, concat_axis=0, tiled=True)  82.7 us
    pallas_call x1, Pallas kernels, on_device(): pl.pallas_call(analyse_kernel, out_shape=jax.ShapeDtypeStruct((owners, le...  9.81 us
    pallas_call x1, Pallas kernels, on_device(): pl.pallas_call(pack_kernel, out_shape=(jax.ShapeDtypeStruct(block, BF16),...  4.6 us

profile of v4, /device:TPU:1, one launch (start us, length us, event | category | flops | bytes accessed | tf_op | source)
XLA Modules:
  0.0 98.8 jit_solution(990412932144968503)
XLA Ops:
  0.0 4.6 %pack.1 = (bf16[128,41,2,128]{3,2,1,0:T(2,128)(2,1)}, s32[1,128]{1,0:T(1,128)}) custom-call(bf16[128,512]{1,0:T(8,128)(2,1)} %pert_hbm.1, f32[1,128]{1,0:T(1,128)} %bitcast.3, f32[1,128]{1,0:T(1,128)} %bitcast.4, f32[2,128]{1,0:T(2,128)} %loc_hbm.1, s32[2,128]{1,0:T(2,128)} %patch_hbm.1, s32[1,128]{1,0:T(1,128)} %bitcast.5, bf16[128,8,512]{2,1,0:T(8,128)(2,1)} %cols_hbm.1), custom_call_target="tpu_custom_call" | custom-call | tf_op jit(solution)/shard_map/pack/pallas_call | solution.py:261
  4.6 48.4 %all_to_all.10.payload_ref = bf16[128,41,2,128]{3,2,1,0:T(2,128)(2,1)S(1)} all-to-all(bf16[128,41,2,128]{3,2,1,0:T(2,128)(2,1)} %get-tuple-element.8), channel_id=1, replica_groups=mesh['gx'=16,'gy'=8] {'gx','gy'}, dimensions={0} | all-to-all | bytes 5373952 | tf_op jit(solution)/shard_map/all_to_all | solution.py:248
  53.0 9.8 %analyse.1 = bf16[128,8,1024]{2,1,0:T(8,128)(2,1)S(1)} custom-call(bf16[128,41,2,128]{3,2,1,0:T(2,128)(2,1)S(1)} %all_to_all.10.payload_ref), custom_call_target="tpu_custom_call" | custom-call | tf_op jit(solution)/shard_map/analyse/pallas_call | solution.py:296
  62.8 0.0 copy-start
  62.8 34.4 %all_to_all.11.cols_ref = bf16[128,8,1024]{2,1,0:T(8,128)(2,1)S(1)} all-to-all(bf16[128,8,1024]{2,1,0:T(8,128)(2,1)S(1)} %analyse.1), channel_id=1, replica_groups=mesh['gx'=16,'gy'=8] {'gx','gy'}, dimensions={0} | all-to-all | bytes 4194304 | tf_op jit(solution)/shard_map/all_to_all | solution.py:248
  97.2 0.0 copy-done
  97.2 1.7 %unpack.1 = bf16[128,8,512]{2,1,0:T(8,128)(2,1)} custom-call(s32[1,128]{1,0:T(1,128)S(1)} %copy-done, bf16[128,8,1024]{2,1,0:T(8,128)(2,1)S(1)} %all_to_all.11.cols_ref), custom_call_target="tpu_custom_call" | custom-call | tf_op jit(solution)/shard_map/unpack/pallas_call | solution.py:307
Async XLA Ops:
  62.8 34.4 %copy-start = (s32[1,128]{1,0:T(1,128)S(1)}, s32[1,128]{1,0:T(1,128)}, u32[]{:S(2)}) copy-start(s32[1,128]{1,0:T(1,128)} %get-tuple-element.7.slot_ref) | copy-start | bytes 1540

commit v5 on v4

--- a/solution.py
+++ b/solution.py
@@ -18,7 +18,7 @@
 COL_ROWS = (0, 48)
 OBS_ROWS = 32
 META_ROWS = 80
-BLOCK_ROWS = 82
+BLOCK_ROWS = 84
 
 
 def ranks(owner, owners):
@@ -120,10 +120,10 @@
 
         def put(i, carry):
             for place in range(CAP):
-                column = held_cols[held_order[0, CAP * i + place]]
-                for group in range(GROUPS):
-                    first = COL_ROWS[place] + 8 * group
-                    block_ref[i, first : first + 8, :] = column[:, group * LANES : (group + 1) * LANES]
+                column = held_cols[held_order[0, CAP * i + place]].astype(F32)
+                column = [column[:, j * LANES : (j + 1) * LANES] for j in range(GROUPS)]
+                column = jnp.concatenate(column, axis=0).astype(BF16)
+                block_ref[i, COL_ROWS[place] : COL_ROWS[place] + 8 * GROUPS, :] = column
             return carry
 
         lax.fori_loop(chunk * block, (chunk + 1) * block, put, 0, unroll=8)
@@ -186,15 +186,22 @@
     sublane = lax.broadcasted_iota(jnp.int32, (half, 8, LANES), 1)
     lane = lax.broadcasted_iota(jnp.int32, (half, 8, LANES), 2)
 
+    lower = block_ref[:half, OBS_ROWS : OBS_ROWS + 16, :].astype(F32)
+    lower_odd = block_ref[:half, OBS_ROWS + OCAP : OBS_ROWS + OCAP + 16, :].astype(F32)
+    upper = block_ref[half:, OBS_ROWS : OBS_ROWS + 16, :].astype(F32)
+    upper_odd = block_ref[half:, OBS_ROWS - OCAP : OBS_ROWS - OCAP + 16, :].astype(F32)
+
     def together(first):
-        lower = block_ref[:half, first : first + 8, :].astype(F32)
-        upper = block_ref[half:, first - OCAP : first - OCAP + 8, :].astype(F32)
-        return jnp.where(sublane < OCAP, lower, upper).reshape(half * 8, LANES)
+        return jnp.where(
+            sublane < OCAP,
+            lower[:, first : first + 8] if first % 8 == 0 else lower_odd[:, first - OCAP : first + OCAP],
+            upper_odd[:, first : first + 8] if first % 8 == 0 else upper[:, first - OCAP : first + OCAP],
+        ).reshape(half * 8, LANES)
 
     row_meta = jnp.where(sublane < OCAP, meta[:half], meta[half:])
     row_meta = jnp.where((lane & (OCAP - 1)) == (sublane & (OCAP - 1)), row_meta, 0.0)
     row_meta = row_meta.reshape(half * 8, LANES)
-    rows = jnp.concatenate([together(OBS_ROWS + OCAP * j) for j in range(GROUPS)] + [row_meta], axis=1)
+    rows = jnp.concatenate([together(OCAP * j) for j in range(GROUPS)] + [row_meta], axis=1)
     diagonal = lax.broadcasted_iota(jnp.int32, (members, members), 0) == lax.broadcasted_iota(
         jnp.int32, (members, members), 1
     )
@@ -231,10 +238,8 @@
         weights_ref[patch] = (root * inverse + mean_weight).astype(BF16)
 
     for place in range(CAP):
-        groups = [
-            block_ref[:, COL_ROWS[place] + 8 * j : COL_ROWS[place] + 8 * j + 8, :].astype(F32) for j in range(GROUPS)
-        ]
-        widened = jnp.concatenate(groups, axis=2)
+        widened = block_ref[:, COL_ROWS[place] : COL_ROWS[place] + 8 * GROUPS, :].astype(F32)
+        widened = jnp.concatenate([widened[:, 8 * j : 8 * j + 8, :] for j in range(GROUPS)], axis=2)
         mean = jnp.mean(widened, axis=-1, keepdims=True)
         spread = (widened - mean).reshape(sources * levels, members).astype(BF16)
         first = jnp.dot(spread, weights_ref[0], preferred_element_type=F32)
@@ -257,7 +262,7 @@
     owners = lax.axis_size(AXES)
     cols, levels, members = background.shape
     obs = obs_pert.shape[0]
-    block = (owners, BLOCK_ROWS // 2, 2, LANES)
+    block = (owners, BLOCK_ROWS // 4, 4, LANES)
     payload, col_slot = pl.pallas_call(
         pack_kernel,
         out_shape=(

time: 99.1 us -> 98.1 us (0.990)
  Pallas kernels: 16.1 us -> 14.4 us
    pallas_call x1, Pallas kernels: 9.81 us -> 8.77 us  [on_device(): pl.pallas_call(analyse_kernel, out_shape=jax.ShapeDtypeStruct((owners, le...]
where the time goes in v5:
time: 98.1 us; the launch traced here: 97.9 us
  blocking collectives  83.5 us (85%)
  Pallas kernels  14.4 us (15%)
    all_to_all x2, blocking collectives, exchange(): return lax.all_to_all(x, AXES, split_axis=0, concat_axis=0, tiled=True)  83.5 us
    pallas_call x1, Pallas kernels, on_device(): pl.pallas_call(analyse_kernel, out_shape=jax.ShapeDtypeStruct((owners, le...  8.77 us
    pallas_call x1, Pallas kernels, on_device(): pl.pallas_call(pack_kernel, out_shape=(jax.ShapeDtypeStruct(block, BF16),...  3.99 us

profile of v5, /device:TPU:1, one launch (start us, length us, event | category | flops | bytes accessed | tf_op | source)
XLA Modules:
  0.0 97.9 jit_solution(4862661030506327664)
XLA Ops:
  0.0 4.0 %pack.1 = (bf16[128,21,4,128]{3,2,1,0:T(4,128)(2,1)}, s32[1,128]{1,0:T(1,128)}) custom-call(bf16[128,512]{1,0:T(8,128)(2,1)} %pert_hbm.1, f32[1,128]{1,0:T(1,128)} %bitcast.3, f32[1,128]{1,0:T(1,128)} %bitcast.4, f32[2,128]{1,0:T(2,128)} %loc_hbm.1, s32[2,128]{1,0:T(2,128)} %patch_hbm.1, s32[1,128]{1,0:T(1,128)} %bitcast.5, bf16[128,8,512]{2,1,0:T(8,128)(2,1)} %cols_hbm.1), custom_call_target="tpu_custom_call" | custom-call | tf_op jit(solution)/shard_map/pack/pallas_call | solution.py:266
  4.0 49.1 %all_to_all.10.payload_ref = bf16[128,21,4,128]{3,2,1,0:T(4,128)(2,1)S(1)} all-to-all(bf16[128,21,4,128]{3,2,1,0:T(4,128)(2,1)} %get-tuple-element.8), channel_id=1, replica_groups=mesh['gx'=16,'gy'=8] {'gx','gy'}, dimensions={0} | all-to-all | bytes 5505024 | tf_op jit(solution)/shard_map/all_to_all | solution.py:253
  53.1 8.8 %analyse.1 = bf16[128,8,1024]{2,1,0:T(8,128)(2,1)S(1)} custom-call(bf16[128,21,4,128]{3,2,1,0:T(4,128)(2,1)S(1)} %all_to_all.10.payload_ref), custom_call_target="tpu_custom_call" | custom-call | tf_op jit(solution)/shard_map/analyse/pallas_call | solution.py:301
  61.9 0.0 copy-start
  61.9 34.4 %all_to_all.11.cols_ref = bf16[128,8,1024]{2,1,0:T(8,128)(2,1)S(1)} all-to-all(bf16[128,8,1024]{2,1,0:T(8,128)(2,1)S(1)} %analyse.1), channel_id=1, replica_groups=mesh['gx'=16,'gy'=8] {'gx','gy'}, dimensions={0} | all-to-all | bytes 4194304 | tf_op jit(solution)/shard_map/all_to_all | solution.py:253
  96.2 0.0 copy-done
  96.3 1.7 %unpack.1 = bf16[128,8,512]{2,1,0:T(8,128)(2,1)} custom-call(s32[1,128]{1,0:T(1,128)S(1)} %copy-done, bf16[128,8,1024]{2,1,0:T(8,128)(2,1)S(1)} %all_to_all.11.cols_ref), custom_call_target="tpu_custom_call" | custom-call | tf_op jit(solution)/shard_map/unpack/pallas_call | solution.py:312
Async XLA Ops:
  61.9 34.4 %copy-start = (s32[1,128]{1,0:T(1,128)S(1)}, s32[1,128]{1,0:T(1,128)}, u32[]{:S(2)}) copy-start(s32[1,128]{1,0:T(1,128)} %get-tuple-element.7.slot_ref) | copy-start | bytes 1540

commit v6 on v5

--- a/solution.py
+++ b/solution.py
@@ -156,7 +156,11 @@
 
 
 def product(a, b):
-    return jnp.dot(a.astype(BF16), b.astype(BF16), preferred_element_type=F32)
+    a, b = a.astype(BF16), b.astype(BF16)
+    half = a.shape[0] // 2
+    top = jnp.dot(a[:half], b, preferred_element_type=F32)
+    last = jnp.dot(a[half:], b[:, half:], preferred_element_type=F32)
+    return jnp.concatenate([top, jnp.concatenate([top[:, half:].T, last], axis=1)], axis=0)
 
 
 def products(a, b):

time: 98.1 us -> 97.6 us (level)
  no operation moved by 1% of the time
where the time goes in v6:
time: 97.6 us; the launch traced here: 97.4 us
  blocking collectives  83.5 us (86%)
  Pallas kernels  13.9 us (14%)
    all_to_all x2, blocking collectives, exchange(): return lax.all_to_all(x, AXES, split_axis=0, concat_axis=0, tiled=True)  83.5 us
    pallas_call x1, Pallas kernels, on_device(): pl.pallas_call(analyse_kernel, out_shape=jax.ShapeDtypeStruct((owners, le...  8.27 us
    pallas_call x1, Pallas kernels, on_device(): pl.pallas_call(pack_kernel, out_shape=(jax.ShapeDtypeStruct(block, BF16),...  3.99 us

profile of v6, /device:TPU:1, one launch (start us, length us, event | category | flops | bytes accessed | tf_op | source)
XLA Modules:
  0.0 97.4 jit_solution(3414497062446598201)
XLA Ops:
  0.0 4.0 %pack.1 = (bf16[128,21,4,128]{3,2,1,0:T(4,128)(2,1)}, s32[1,128]{1,0:T(1,128)}) custom-call(bf16[128,512]{1,0:T(8,128)(2,1)} %pert_hbm.1, f32[1,128]{1,0:T(1,128)} %bitcast.3, f32[1,128]{1,0:T(1,128)} %bitcast.4, f32[2,128]{1,0:T(2,128)} %loc_hbm.1, s32[2,128]{1,0:T(2,128)} %patch_hbm.1, s32[1,128]{1,0:T(1,128)} %bitcast.5, bf16[128,8,512]{2,1,0:T(8,128)(2,1)} %cols_hbm.1), custom_call_target="tpu_custom_call" | custom-call | tf_op jit(solution)/shard_map/pack/pallas_call | solution.py:270
  4.0 49.1 %all_to_all.10.payload_ref = bf16[128,21,4,128]{3,2,1,0:T(4,128)(2,1)S(1)} all-to-all(bf16[128,21,4,128]{3,2,1,0:T(4,128)(2,1)} %get-tuple-element.8), channel_id=1, replica_groups=mesh['gx'=16,'gy'=8] {'gx','gy'}, dimensions={0} | all-to-all | bytes 5505024 | tf_op jit(solution)/shard_map/all_to_all | solution.py:257
  53.1 8.3 %analyse.1 = bf16[128,8,1024]{2,1,0:T(8,128)(2,1)S(1)} custom-call(bf16[128,21,4,128]{3,2,1,0:T(4,128)(2,1)S(1)} %all_to_all.10.payload_ref), custom_call_target="tpu_custom_call" | custom-call | tf_op jit(solution)/shard_map/analyse/pallas_call | solution.py:305
  61.3 0.0 copy-start
  61.4 34.4 %all_to_all.11.cols_ref = bf16[128,8,1024]{2,1,0:T(8,128)(2,1)S(1)} all-to-all(bf16[128,8,1024]{2,1,0:T(8,128)(2,1)S(1)} %analyse.1), channel_id=1, replica_groups=mesh['gx'=16,'gy'=8] {'gx','gy'}, dimensions={0} | all-to-all | bytes 4194304 | tf_op jit(solution)/shard_map/all_to_all | solution.py:257
  95.7 0.0 copy-done
  95.7 1.7 %unpack.1 = bf16[128,8,512]{2,1,0:T(8,128)(2,1)} custom-call(s32[1,128]{1,0:T(1,128)S(1)} %copy-done, bf16[128,8,1024]{2,1,0:T(8,128)(2,1)S(1)} %all_to_all.11.cols_ref), custom_call_target="tpu_custom_call" | custom-call | tf_op jit(solution)/shard_map/unpack/pallas_call | solution.py:316
Async XLA Ops:
  61.3 34.4 %copy-start = (s32[1,128]{1,0:T(1,128)S(1)}, s32[1,128]{1,0:T(1,128)}, u32[]{:S(2)}) copy-start(s32[1,128]{1,0:T(1,128)} %get-tuple-element.7.slot_ref) | copy-start | bytes 1540

commit v7 on v6

--- a/solution.py
+++ b/solution.py
@@ -205,17 +205,19 @@
     row_meta = jnp.where(sublane < OCAP, meta[:half], meta[half:])
     row_meta = jnp.where((lane & (OCAP - 1)) == (sublane & (OCAP - 1)), row_meta, 0.0)
     row_meta = row_meta.reshape(half * 8, LANES)
-    rows = jnp.concatenate([together(OCAP * j) for j in range(GROUPS)] + [row_meta], axis=1)
+    rows = jnp.concatenate([together(OCAP * j) for j in range(GROUPS)], axis=1)
+    lifted = jnp.sum(jnp.where(lane < OCAP, row_meta.reshape(half, 8, LANES), 0.0), axis=2, keepdims=True)
+    lifted = jnp.broadcast_to(lifted, (half, 8, LANES)).reshape(half * 8, LANES)
     diagonal = lax.broadcasted_iota(jnp.int32, (members, members), 0) == lax.broadcasted_iota(
         jnp.int32, (members, members), 1
     )
     both = range(PATCH_DEV)
     flipped = rows.T
-    tag = jnp.sum(flipped[members + OCAP : members + 2 * OCAP], axis=0, keepdims=True)
-    rows = rows.astype(BF16)
+    tag = jnp.sum(row_meta.T[OCAP : 2 * OCAP], axis=0, keepdims=True)
+    rows = jnp.concatenate([rows, lifted], axis=1).astype(BF16)
     wide = [
         jnp.dot(
-            jnp.where(tag == patch + 1, flipped[:members], 0.0).astype(BF16), rows, preferred_element_type=F32
+            jnp.where(tag == patch + 1, flipped, 0.0).astype(BF16), rows, preferred_element_type=F32
         )
         for patch in both
     ]
@@ -235,7 +237,7 @@
     for patch in both:
         inverse = last[patch] + z[patch] * f[patch] + y[patch] * d[patch]
         inverse += jnp.where(diagonal, z[patch] * y[patch], 0.0)
-        pull = jnp.sum(wide[patch][:, members : members + OCAP], axis=1, keepdims=True)
+        pull = jnp.concatenate([wide[patch][:, members:]] * GROUPS, axis=1)
         once = jnp.sum(inverse * pull, axis=0, keepdims=True)
         mean_weight = jnp.sum(inverse * once, axis=1, keepdims=True) * scale[patch]
         root = jnp.sqrt((members - 1) * scale[patch])

time: 97.6 us -> 97.5 us (level)
  no operation moved by 1% of the time
where the time goes in v7:
time: 97.5 us; the launch traced here: 97.3 us
  blocking collectives  83.5 us (86%)
  Pallas kernels  13.8 us (14%)
    all_to_all x2, blocking collectives, exchange(): return lax.all_to_all(x, AXES, split_axis=0, concat_axis=0, tiled=True)  83.5 us
    pallas_call x1, Pallas kernels, on_device(): pl.pallas_call(analyse_kernel, out_shape=jax.ShapeDtypeStruct((owners, le...  8.11 us
    pallas_call x1, Pallas kernels, on_device(): pl.pallas_call(pack_kernel, out_shape=(jax.ShapeDtypeStruct(block, BF16),...  3.99 us

profile of v7, /device:TPU:1, one launch (start us, length us, event | category | flops | bytes accessed | tf_op | source)
XLA Modules:
  0.0 97.3 jit_solution(10131051927036772561)
XLA Ops:
  0.0 4.0 %pack.1 = (bf16[128,21,4,128]{3,2,1,0:T(4,128)(2,1)}, s32[1,128]{1,0:T(1,128)}) custom-call(bf16[128,512]{1,0:T(8,128)(2,1)} %pert_hbm.1, f32[1,128]{1,0:T(1,128)} %bitcast.3, f32[1,128]{1,0:T(1,128)} %bitcast.4, f32[2,128]{1,0:T(2,128)} %loc_hbm.1, s32[2,128]{1,0:T(2,128)} %patch_hbm.1, s32[1,128]{1,0:T(1,128)} %bitcast.5, bf16[128,8,512]{2,1,0:T(8,128)(2,1)} %cols_hbm.1), custom_call_target="tpu_custom_call" | custom-call | tf_op jit(solution)/shard_map/pack/pallas_call | solution.py:272
  4.0 49.1 %all_to_all.10.payload_ref = bf16[128,21,4,128]{3,2,1,0:T(4,128)(2,1)S(1)} all-to-all(bf16[128,21,4,128]{3,2,1,0:T(4,128)(2,1)} %get-tuple-element.8), channel_id=1, replica_groups=mesh['gx'=16,'gy'=8] {'gx','gy'}, dimensions={0} | all-to-all | bytes 5505024 | tf_op jit(solution)/shard_map/all_to_all | solution.py:259
  53.1 8.1 %analyse.1 = bf16[128,8,1024]{2,1,0:T(8,128)(2,1)S(1)} custom-call(bf16[128,21,4,128]{3,2,1,0:T(4,128)(2,1)S(1)} %all_to_all.10.payload_ref), custom_call_target="tpu_custom_call" | custom-call | tf_op jit(solution)/shard_map/analyse/pallas_call | solution.py:307
  61.2 0.0 copy-start
  61.2 34.4 %all_to_all.11.cols_ref = bf16[128,8,1024]{2,1,0:T(8,128)(2,1)S(1)} all-to-all(bf16[128,8,1024]{2,1,0:T(8,128)(2,1)S(1)} %analyse.1), channel_id=1, replica_groups=mesh['gx'=16,'gy'=8] {'gx','gy'}, dimensions={0} | all-to-all | bytes 4194304 | tf_op jit(solution)/shard_map/all_to_all | solution.py:259
  95.6 0.0 copy-done
  95.6 1.7 %unpack.1 = bf16[128,8,512]{2,1,0:T(8,128)(2,1)} custom-call(s32[1,128]{1,0:T(1,128)S(1)} %copy-done, bf16[128,8,1024]{2,1,0:T(8,128)(2,1)S(1)} %all_to_all.11.cols_ref), custom_call_target="tpu_custom_call" | custom-call | tf_op jit(solution)/shard_map/unpack/pallas_call | solution.py:318
Async XLA Ops:
  61.2 34.4 %copy-start = (s32[1,128]{1,0:T(1,128)S(1)}, s32[1,128]{1,0:T(1,128)}, u32[]{:S(2)}) copy-start(s32[1,128]{1,0:T(1,128)} %get-tuple-element.7.slot_ref) | copy-start | bytes 1540
